TPU v7x, 128 devices: a whole 4x4x4 slice. The times are simulated.
128 devices in a mesh: gx: 8 (over z, core), gy: 16 (over x, y).
Axes of the slice: x: 4, y: 4, z: 4, core: 2. Of those that a mesh axis runs over, the one named last changes fastest.
Arguments:
- soil_state: float32 [9, 64, 64, 2048], P(None, 'gx', None, 'gy'), may hold values from -6 to 6
- material: bfloat16 [3, 64, 64, 2048], P(None, 'gx', None, 'gy'), may hold values from 0.5 to 1.5
- dashpot: float32 [64, 2048], P('gx', 'gy'), may hold values from 0.02 to 0.2
- foot_cells: int32 [1024, 128], P(('gx', 'gy')), may hold values from 0 to 1023, as said below
- owner_table: int32 [3, 128], replicated, may hold values from 0 to 127, each once within a row
- stiffness: float32 [12, 12, 262144], P(None, None, ('gx', 'gy')), as said below
- beam_links: int32 [2, 262144], P(None, ('gx', 'gy')), may hold values from 0 to 127
- beam_count: int32 [1024], P(('gx', 'gy')), may hold values from 128 to 256
- inverse_mass: float32 [6, 131072], P(None, ('gx', 'gy')), may hold values from 0.25 to 1
- frame_displacement: float32 [6, 131072], P(None, ('gx', 'gy')), may hold values from -2 to 2
- frame_velocity: float32 [6, 131072], P(None, ('gx', 'gy')), may hold values from -2 to 2
Outputs:
- soil_after: float32 [9, 64, 64, 2048], P(None, 'gx', None, 'gy')
- base_force: float32 [3, 64, 2048], P(None, 'gx', 'gy')
- displacement_after: float32 [6, 131072], P(None, ('gx', 'gy'))
- velocity_after: float32 [6, 131072], P(None, ('gx', 'gy'))
Inputs may be any that keep to these rules, and one draw needn't show every extreme that they name: `foot_cells`: the 8 rows of each device list each of its 1024 local surface cells (x-major) exactly once. `stiffness`: each beam's 12 x 12 matrix is symmetric.
All inputs are finite; a program needn't handle non-finite values.
Results may differ from a plain program's by a relative error of at most 0.0003.
Values sent between devices are 32-bit elements; how exact they have to be, the bound alone decides.
A program may use at most 128 MiB of HBM per device.

v0:
```python
import functools

import jax
import jax.numpy as jnp
from jax import lax
from jax.experimental import pallas as pl
from jax.experimental.pallas import tpu as pltpu
from jax.sharding import PartitionSpec as P

GROUPS = 4
FRAME_STEPS = 4
NEAR = 9.0 / 8.0
FAR = -1.0 / 24.0
TIME_SOIL = 0.18
TIME_FRAME = 0.05
MESH = pl.DeviceIdType.MESH
ROW = 8
COL = 2
F32 = jnp.float32
BF16 = jnp.bfloat16

VX, VY, VZ, SXX, SYY, SZZ, SXY, SXZ, SYZ = range(9)


def lane_gather(values, index):
    return lax.gather(
        values,
        index[:, :, None],
        lax.GatherDimensionNumbers(
            offset_dims=(),
            collapsed_slice_dims=(1,),
            start_index_map=(1,),
            operand_batching_dims=(0,),
            start_indices_batching_dims=(0,),
        ),
        (1, 1),
        mode=lax.GatherScatterMode.PROMISE_IN_BOUNDS,
    )


def iota(shape, dim):
    return lax.broadcasted_iota(jnp.int32, shape, dim)


def stencil(near_high, near_low, far_high, far_low):
    return NEAR * (near_high - near_low) + FAR * (far_high - far_low)


def rolled(value, shift):
    return pltpu.roll(value, shift, 1)


def kernel(
    n_gx,
    n_gy,
    soil,
    material,
    dashpot,
    foot,
    table,
    stiff,
    links,
    count,
    inverse_mass,
    frame_disp,
    frame_vel,
    soil_out,
    force_out,
    disp_out,
    vel_out,
    first,
    vel_a,
    str_a,
    vel_b,
    str_b,
    raw,
    coef,
    matrix,
    spread,
    pack_up,
    pack_down,
    from_low,
    from_high,
    owners,
    bids,
    damp_vec,
    disp,
    vel,
    imass,
    foot_sum,
    index,
    row_buf,
    rows_all,
    load_sem,
    store_sem,
    x_send,
    x_recv,
    y_send,
    y_recv,
    a_send,
    a_recv,
    b_send,
    b_recv,
):
    gx = lax.axis_index("gx")
    gy = lax.axis_index("gy")
    me = gx * n_gy + gy
    n_dev = n_gx * n_gy
    gx_up, gx_down = lax.rem(gx + 1, n_gx), lax.rem(gx + n_gx - 1, n_gx)
    gy_up, gy_down = lax.rem(gy + 1, n_gy), lax.rem(gy + n_gy - 1, n_gy)
    cells_x, cells_z, cells_y = soil.shape[1:]
    tiles_z = cells_z // 8
    buildings = foot.shape[0]
    inner = pl.ds(COL, cells_x)
    rows = pl.ds(ROW, cells_z)

    def load(k, source, target):
        copy = pltpu.make_async_copy(source, target, load_sem.at[k])
        copy.start()
        return copy

    load_stress = load(0, soil.at[pl.ds(SXX, 6)], first.at[pl.ds(SXX, 6), inner, rows])
    load_velocity = load(1, soil.at[pl.ds(0, 3)], first.at[pl.ds(0, 3), inner, rows])
    load_material = load(2, material, raw)
    load_matrix = load(3, stiff, matrix)

    barrier = pltpu.get_barrier_semaphore()
    for k in range(1, n_gx):
        pl.semaphore_signal(
            barrier, inc=1, device_id={"gx": lax.rem(gx + k, n_gx)}, device_id_type=MESH
        )
    for k in range(1, n_gy):
        pl.semaphore_signal(
            barrier, inc=1, device_id={"gy": lax.rem(gy + k, n_gy)}, device_id_type=MESH
        )

    zero_tile = jnp.zeros((8, cells_y), F32)

    def clear(x, carry):
        for ref, members in (
            (first, (SZZ, SXZ, SYZ)),
            (vel_a, (0, 1, 2)),
            (str_a, (2, 4, 5)),
            (vel_b, (0, 1, 2)),
        ):
            for member in members:
                ref[member, x, pl.ds(0, 8), :] = zero_tile
                ref[member, x, pl.ds(ROW + cells_z, 8), :] = zero_tile
        return carry

    lax.fori_loop(COL, COL + cells_x, clear, 0)

    pl.semaphore_wait(barrier, n_gx + n_gy - 2)

    def remote(source, target, send, recv, device):
        copy = pltpu.make_async_remote_copy(
            src_ref=source,
            dst_ref=target,
            send_sem=send,
            recv_sem=recv,
            device_id=device,
            device_id_type=MESH,
        )
        copy.start()
        return copy

    def send_x(stage, source, start, target, groups, up, down):
        copies = []
        for k, (origin, member, size) in enumerate(groups):
            ids, into = pl.ds(origin, size), pl.ds(member, size)
            copies.append(
                remote(
                    source.at[ids, pl.ds(start + cells_x - up, up), rows if start else pl.ds(0, cells_z)],
                    target.at[into, pl.ds(COL - up, up), rows],
                    x_send.at[stage, k, 0],
                    x_recv.at[stage, k, 0],
                    {"gx": gx_up},
                )
            )
            copies.append(
                remote(
                    source.at[ids, pl.ds(start, down), rows if start else pl.ds(0, cells_z)],
                    target.at[into, pl.ds(COL + cells_x, down), rows],
                    x_send.at[stage, k, 1],
                    x_recv.at[stage, k, 1],
                    {"gx": gx_down},
                )
            )
        return copies

    def send_y(stage):
        return [
            remote(
                pack_up.at[stage],
                from_low.at[stage],
                y_send.at[stage, 0],
                y_recv.at[stage, 0],
                {"gy": gy_up},
            ),
            remote(
                pack_down.at[stage],
                from_high.at[stage],
                y_send.at[stage, 1],
                y_recv.at[stage, 1],
                {"gy": gy_down},
            ),
        ]

    def finish(copies):
        for copy in copies:
            copy.wait()

    def outside_zero_x(ref, members, low, high):
        @pl.when(gx == 0)
        def _():
            for member in members:
                for layer in range(low):
                    ref[member, COL - 1 - layer, rows, :] = jnp.zeros((cells_z, cells_y), F32)

        @pl.when(gx == n_gx - 1)
        def _():
            for member in members:
                for layer in range(high):
                    ref[member, COL + cells_x + layer, rows, :] = jnp.zeros((cells_z, cells_y), F32)

    def outside_zero_y(stage):
        @pl.when(gy == 0)
        def _():
            from_low[stage] = jnp.zeros(from_low.shape[1:], F32)

        @pl.when(gy == n_gy - 1)
        def _():
            from_high[stage] = jnp.zeros(from_high.shape[1:], F32)

    lane = iota((8, cells_y), 1)
    lane_single, lane_double = lane, lane // 2

    def pack(packed, values, tile, up):
        ups, downs = packed
        if up == 2:
            up_mask, down_mask = lane_double == tile, lane_single == tile
            up_shift, down_shift = lax.rem(2 * tile + 2, 128), tile
        else:
            up_mask, down_mask = lane_single == tile, lane_double == tile
            up_shift, down_shift = tile + 1, 2 * tile
        ups = tuple(
            jnp.where(up_mask, rolled(value, up_shift), old) for value, old in zip(values, ups)
        )
        downs = tuple(
            jnp.where(down_mask, rolled(value, down_shift), old) for value, old in zip(values, downs)
        )
        return ups, downs

    nothing = (tuple([zero_tile] * 3), tuple([zero_tile] * 3))

    def keep_packed(stage, packed):
        for k in range(3):
            pack_up[stage, k] = packed[0][k]
            pack_down[stage, k] = packed[1][k]

    def along_y(value, stage, k, tile, forward):
        if forward:
            low = jnp.where(
                lane == cells_y - 1, rolled(from_low[stage, k], lax.rem(127 - tile, 128)), value
            )
            beyond = rolled(from_high[stage, k], lax.rem(128 - 2 * tile, 128))
            near, far = jnp.where(lane < 1, beyond, value), jnp.where(lane < 2, beyond, value)
            return stencil(rolled(near, 127), value, rolled(far, 126), rolled(low, 1))
        beyond = rolled(from_low[stage, k], lax.rem(254 - 2 * tile, 128))
        near = jnp.where(lane == cells_y - 1, beyond, value)
        far = jnp.where(lane >= cells_y - 2, beyond, value)
        high = jnp.where(lane < 1, rolled(from_high[stage, k], lax.rem(128 - tile, 128)), value)
        return stencil(value, rolled(near, 1), rolled(high, 127), rolled(far, 2))

    def at(ref, member, x, row):
        return ref[member, x, pl.ds(row, 8), :]

    def along_x(ref, member, x, row, forward):
        shift = 1 if forward else 0
        return stencil(
            at(ref, member, x + shift, row),
            at(ref, member, x + shift - 1, row),
            at(ref, member, x + shift + 1, row),
            at(ref, member, x + shift - 2, row),
        )

    def along_z(ref, member, x, row, forward):
        shift = 1 if forward else 0
        return stencil(
            at(ref, member, x, row + shift),
            at(ref, member, x, row + shift - 1),
            at(ref, member, x, row + shift + 1),
            at(ref, member, x, row + shift - 2),
        )

    def velocity_layers(stage, stress, base, old, new, begin, end, packed):
        sxx, syy, szz, sxy, sxz, syz = range(base, base + 6)

        def layer(i, packed):
            cell = lax.rem(i + cells_x - 1, cells_x)
            x = cell + COL
            for z in range(tiles_z):
                row = ROW + 8 * z
                tile = cell * tiles_z + z
                y_of = [
                    along_y(at(stress, member, x, row), stage, k, tile, False)
                    for k, member in enumerate((sxy, syy, syz))
                ]
                accel = (
                    along_x(stress, sxx, x, row, False) + y_of[0] + along_z(stress, sxz, x, row, False),
                    along_x(stress, sxy, x, row, False) + y_of[1] + along_z(stress, syz, x, row, False),
                    along_x(stress, sxz, x, row, False) + y_of[2] + along_z(stress, szz, x, row, False),
                )
                density = coef[0, cell, pl.ds(8 * z, 8), :]
                after = [at(old, k, x, row) + density * accel[k] for k in range(3)]
                for k in range(3):
                    new[k, x, pl.ds(row, 8), :] = after[k]
                packed = pack(packed, after, tile, 1)
            return packed

        return lax.fori_loop(begin, end, layer, packed)

    def stress_layers(stage, moving, stress, base, new, new_x, new_row, begin, end, packed):
        def layer(i, packed):
            cell = lax.rem(i + cells_x - 2, cells_x)
            x = cell + COL
            for z in range(tiles_z):
                row = ROW + 8 * z
                tile = cell * tiles_z + z
                y_of = [
                    along_y(at(moving, k, x, row), stage, k, tile, True) for k in range(3)
                ]
                x_of = [along_x(moving, k, x, row, True) for k in range(3)]
                z_of = [along_z(moving, k, x, row, True) for k in range(3)]
                lame = coef[1, cell, pl.ds(8 * z, 8), :]
                shear = coef[2, cell, pl.ds(8 * z, 8), :]
                volume = lame * (x_of[0] + y_of[1] + z_of[2])
                twice = shear + shear
                change = (
                    volume + twice * x_of[0],
                    volume + twice * y_of[1],
                    volume + twice * z_of[2],
                    shear * (y_of[0] + x_of[1]),
                    shear * (z_of[0] + x_of[2]),
                    shear * (z_of[1] + y_of[2]),
                )
                after = [at(stress, base + k, x, row) + change[k] for k in range(6)]
                for k in range(6):
                    new[k, cell + new_x, pl.ds(new_row + 8 * z, 8), :] = after[k]
                if packed is not None:
                    packed = pack(packed, (after[3], after[1], after[5]), tile, 2)
            return packed

        if packed is None:

            def bare(i, carry):
                layer(i, None)
                return carry

            lax.fori_loop(begin, end, bare, 0)
            return None
        return lax.fori_loop(begin, end, layer, packed)

    stress_groups = ((SXX, SXX, 1), (SXY, SXY, 2))
    inner_groups = ((0, 0, 1), (3, 3, 2))
    move_groups = ((0, 0, 3),)

    sent = send_x(0, soil, 0, first, stress_groups, 2, 1)
    load_stress.wait()

    def pack_first(cell, packed):
        for z in range(tiles_z):
            values = [at(first, k, cell + COL, ROW + 8 * z) for k in (SXY, SYY, SYZ)]
            packed = pack(packed, values, cell * tiles_z + z, 2)
        return packed

    keep_packed(0, lax.fori_loop(0, cells_x, pack_first, nothing))
    sent += send_y(0)

    load_material.wait()

    def widen(cell, carry):
        for k in range(3):
            coef[k, cell] = TIME_SOIL * raw[k, cell].astype(F32)
        return carry

    lax.fori_loop(0, cells_x, widen, 0)
    load_velocity.wait()

    finish(sent)
    outside_zero_x(first, (SXX, SXY, SXZ), 2, 1)
    outside_zero_y(0)

    packed = velocity_layers(0, first, SXX, first, vel_a, 0, 3, nothing)
    sent = send_x(1, vel_a, COL, vel_a, move_groups, 1, 2)
    packed = velocity_layers(0, first, SXX, first, vel_a, 3, cells_x, packed)
    keep_packed(1, packed)
    sent += send_y(1)

    big = (128, 128)
    big_lane = iota(big, 1)
    big_lane_f = big_lane.astype(F32)
    small_row = iota((8, 128), 0)
    small_lane = iota((8, 128), 1)

    for b in range(buildings):
        for h in range(2):
            piece = pl.ds(b * 256 + h * 128, 128)
            live = iota((1, 128), 1) + h * 128 < count[b]
            for end in range(2):
                nodes = links[pl.ds(end, 1), piece]
                index[b, h * 2 + end] = jnp.broadcast_to(nodes, (8, 128))
                kept = jnp.where(live, nodes, -1).astype(F32)
                columns = jnp.broadcast_to(kept, big).T
                spread[b, pl.ds(h * 128, 128), pl.ds(end * 128, 128)] = (
                    jnp.where(columns == big_lane_f, 1.0, 0.0).astype(BF16)
                )

    group_of = (iota((n_dev, 128), 1) // 2) % GROUPS
    holder = iota((n_dev, 128), 0)
    for j in range(1, GROUPS):
        entries = table[pl.ds(j - 1, 1), :].astype(F32)
        columns = jnp.broadcast_to(entries, (128, n_dev)).T.astype(jnp.int32)
        holder = jnp.where(group_of == j, columns, holder)
    owners[...] = holder

    bid = jnp.zeros((16, 128), F32)
    for b in range(buildings):
        cell = foot[pl.ds(b, 1), :]
        place_x = jnp.where(iota((16, 128), 0) == cell // cells_y, float(b), 0.0).astype(BF16)
        place_y = jnp.where(iota(big, 0) == cell % cells_y, 1.0, 0.0).astype(BF16)
        bid += lax.dot_general(
            place_x, place_y, (((1,), (1,)), ((), ())), preferred_element_type=F32
        )
    bids[...] = bid[0:8].astype(jnp.int32)

    blank = jnp.zeros((2, 128), F32)
    for b in range(buildings):
        piece = pl.ds(b * 128, 128)
        disp[b] = jnp.concatenate([frame_disp[:, piece], blank], 0)
        vel[b] = jnp.concatenate([frame_vel[:, piece], blank], 0)
        imass[b] = TIME_FRAME * jnp.concatenate([inverse_mass[:, piece], blank], 0)
        foot_sum[b] = jnp.zeros((8, 128), F32)

    finish(sent)
    outside_zero_x(vel_a, (0, 1, 2), 1, 2)
    outside_zero_y(1)

    packed = stress_layers(1, vel_a, first, SXX, str_a, COL, ROW, 0, 3, nothing)
    sent = send_x(2, str_a, COL, str_a, inner_groups, 2, 1)
    packed = stress_layers(1, vel_a, first, SXX, str_a, COL, ROW, 3, cells_x, packed)
    keep_packed(2, packed)
    sent += send_y(2)
    finish(sent)
    outside_zero_x(str_a, (0, 3, 4), 2, 1)
    outside_zero_y(2)

    packed = velocity_layers(2, str_a, 0, vel_a, vel_b, 0, 3, nothing)
    sent = send_x(3, vel_b, COL, vel_b, move_groups, 1, 2)
    packed = velocity_layers(2, str_a, 0, vel_a, vel_b, 3, cells_x, packed)
    keep_packed(3, packed)
    sent += send_y(3)

    store_velocity = pltpu.make_async_copy(
        vel_b.at[:, inner, rows], soil_out.at[pl.ds(0, 3)], store_sem.at[0]
    )
    store_velocity.start()

    surface = [vel_b[k, inner, ROW, :] for k in range(3)]
    dash = dashpot[...]
    terms = [dash * surface[0], dash * surface[1], dash * surface[2], dash]
    bid = bids[...]
    sums = [
        jnp.sum(jnp.where(bid == b, term, 0.0), axis=0, keepdims=True)
        for term in terms
        for b in range(buildings)
    ]
    sums = jnp.concatenate(sums + [jnp.zeros((128 - len(sums), 128), F32)], 0)
    mine = jnp.sum(sums.T, axis=0, keepdims=True)

    def gather_rows(turn, value):
        row_buf[turn, gy] = value
        sent = [
            remote(
                row_buf.at[turn, gy],
                row_buf.at[turn, gy],
                a_send.at[turn, k - 1],
                a_recv.at[turn, k - 1],
                {"gy": lax.rem(gy + k, n_gy)},
            )
            for k in range(1, n_gy)
        ]
        finish(sent)
        rows_all[turn, gx] = row_buf[turn].reshape(n_gy, 128)
        return [
            remote(
                rows_all.at[turn, gx],
                rows_all.at[turn, gx],
                b_send.at[turn, k - 1],
                b_recv.at[turn, k - 1],
                {"gx": lax.rem(gx + k, n_gx)},
            )
            for k in range(1, n_gx)
        ]

    gathering = gather_rows(0, mine)

    finish(sent)
    outside_zero_x(vel_b, (0, 1, 2), 1, 2)
    outside_zero_y(3)
    stress_layers(3, vel_b, str_a, 0, str_b, 0, 0, 0, cells_x, None)
    store_stress = pltpu.make_async_copy(str_b, soil_out.at[pl.ds(3, 6)], store_sem.at[1])
    store_stress.start()

    finish(gathering)
    arrived = rows_all[0].reshape(n_dev, 128)
    owned = jnp.sum(jnp.where(owners[...] == me, arrived, 0.0), axis=0, keepdims=True)
    owned = jnp.broadcast_to(owned, (8, 128))

    at_footing = (small_row < 3) & (small_lane == 0)
    load_matrix.wait()
    drives, dampers = [], []
    for b in range(buildings):
        pick = jnp.minimum(small_row * buildings + b, 127)
        drives.append(jnp.where(at_footing, lane_gather(owned, pick), 0.0))
        pick = jnp.full((8, 128), 3 * buildings + b, jnp.int32)
        dampers.append(jnp.where(at_footing, lane_gather(owned, pick), 0.0))
    for b in range(buildings):
        damp_vec[0, b] = drives[b]
        damp_vec[1, b] = dampers[b]

    def frame_step(step, carry):
        for b in range(buildings):
            place = disp[b]
            forces = []
            for h in range(2):
                ends = (
                    lane_gather(place, index[b, h * 2]),
                    lane_gather(place, index[b, h * 2 + 1]),
                )
                piece = pl.ds(b * 256 + h * 128, 128)
                total = None
                for a in range(12):
                    row = ends[a // 6][a % 6 : a % 6 + 1, :]
                    term = matrix[a, :, piece] * row
                    total = term if total is None else total + term
                forces.append(jnp.concatenate([total, jnp.zeros((4, 128), F32)], 0))
            forces = jnp.concatenate(forces, 1)
            high = forces.astype(BF16)
            low = (forces - high.astype(F32)).astype(BF16)
            parts = jnp.dot(
                jnp.concatenate([high, low], 0), spread[b], preferred_element_type=F32
            )
            parts = parts[0:16] + parts[16:32]
            internal = parts[0:8, 0:128] + parts[6:14, 128:256]
            speed = vel[b]
            loads = damp_vec[0, b] - damp_vec[1, b] * speed - internal
            speed = speed + imass[b] * loads
            vel[b] = speed
            disp[b] = place + TIME_FRAME * speed
            foot_sum[b] += speed
        return carry

    lax.fori_loop(0, FRAME_STEPS, frame_step, 0)

    back = jnp.zeros((8, 128), F32)
    for b in range(buildings):
        whole = jnp.broadcast_to(foot_sum[b][:, 0:1], (8, 128))
        back = jnp.where(small_lane == small_row * buildings + b, whole, back)
    back = jnp.where(small_row < 3, back, 0.0)
    gathering = gather_rows(1, jnp.sum(back, axis=0, keepdims=True))
    for b in range(buildings):
        piece = pl.ds(b * 128, 128)
        disp_out[:, piece] = disp[b][0:6]
        vel_out[:, piece] = vel[b][0:6]
    wanted = owners[pl.ds(me, 1), :]
    finish(gathering)
    arrived = rows_all[1].reshape(n_dev, 128)
    held = jnp.where(iota((n_dev, 128), 0) == wanted, arrived, 0.0)
    held = jnp.broadcast_to(jnp.sum(held, axis=0, keepdims=True), (8, 128))
    for k in range(3):
        total = lane_gather(held, bid + k * buildings)
        force_out[k] = dash * (FRAME_STEPS * surface[k] - total)

    finish(sent[:0])
    store_velocity.wait()
    store_stress.wait()


def shards(n_gx, n_gy, *args):
    soil, material, dashpot, foot, table, stiff, links = args[:7]
    cells_x, cells_z, cells_y = soil.shape[1:]
    buildings = foot.shape[0]
    wide = (cells_x + 2 * COL, cells_z + 2 * ROW, cells_y)
    n_dev = n_gx * n_gy
    anywhere = pl.BlockSpec(memory_space=pl.ANY)
    vmem = pl.BlockSpec(memory_space=pltpu.VMEM)
    smem = pl.BlockSpec(memory_space=pltpu.SMEM)
    dma = pltpu.SemaphoreType.DMA
    return pl.pallas_call(
        functools.partial(kernel, n_gx, n_gy),
        out_shape=(
            jax.ShapeDtypeStruct(soil.shape, F32),
            jax.ShapeDtypeStruct((3, cells_x, cells_y), F32),
            jax.ShapeDtypeStruct(args[9].shape, F32),
            jax.ShapeDtypeStruct(args[10].shape, F32),
        ),
        in_specs=[anywhere, anywhere, vmem, vmem, vmem, anywhere, vmem, smem, vmem, vmem, vmem],
        out_specs=(anywhere, vmem, vmem, vmem),
        scratch_shapes=[
            pltpu.VMEM((9,) + wide, F32),
            pltpu.VMEM((3,) + wide, F32),
            pltpu.VMEM((6,) + wide, F32),
            pltpu.VMEM((3,) + wide, F32),
            pltpu.VMEM((6, cells_x, cells_z, cells_y), F32),
            pltpu.VMEM(material.shape, BF16),
            pltpu.VMEM(material.shape, F32),
            pltpu.VMEM(stiff.shape, F32),
            pltpu.VMEM((buildings, 256, 256), BF16),
            pltpu.VMEM((4, 3, 8, 128), F32),
            pltpu.VMEM((4, 3, 8, 128), F32),
            pltpu.VMEM((4, 3, 8, 128), F32),
            pltpu.VMEM((4, 3, 8, 128), F32),
            pltpu.VMEM((n_dev, 128), jnp.int32),
            pltpu.VMEM((8, 128), jnp.int32),
            pltpu.VMEM((2, buildings, 8, 128), F32),
            pltpu.VMEM((buildings, 8, 128), F32),
            pltpu.VMEM((buildings, 8, 128), F32),
            pltpu.VMEM((buildings, 8, 128), F32),
            pltpu.VMEM((buildings, 8, 128), F32),
            pltpu.VMEM((buildings, 4, 8, 128), jnp.int32),
            pltpu.VMEM((2, n_gy, 1, 128), F32),
            pltpu.VMEM((2, n_gx, n_gy, 128), F32),
            dma((4,)),
            dma((2,)),
            dma((4, 2, 2)),
            dma((4, 2, 2)),
            dma((4, 2)),
            dma((4, 2)),
            dma((2, n_gy - 1)),
            dma((2, n_gy - 1)),
            dma((2, n_gx - 1)),
            dma((2, n_gx - 1)),
        ],
        compiler_params=pltpu.CompilerParams(
            collective_id=0, has_side_effects=True, vmem_limit_bytes=48 * 1024 * 1024
        ),
    )(*args)


def solution(mesh):
    placed = (
        P(None, "gx", None, "gy"),
        P(None, "gx", None, "gy"),
        P("gx", "gy"),
        P(("gx", "gy"), None),
        P(),
        P(None, None, ("gx", "gy")),
        P(None, ("gx", "gy")),
        P(("gx", "gy")),
        P(None, ("gx", "gy")),
        P(None, ("gx", "gy")),
        P(None, ("gx", "gy")),
    )
    return jax.shard_map(
        functools.partial(shards, mesh.shape["gx"], mesh.shape["gy"]),
        mesh=mesh,
        in_specs=placed,
        out_specs=(
            P(None, "gx", None, "gy"),
            P(None, "gx", "gy"),
            P(None, ("gx", "gy")),
            P(None, ("gx", "gy")),
        ),
        check_vma=False,
    )
```

profile of v0, /device:TPU:1, one launch (start us, length us, event | category | flops | bytes accessed | tf_op | source)
XLA Modules:
  0.0 61.9 jit_solution(17154679848610468972)
XLA Ops:
  0.6 0.0 copy-start
  0.6 1.4 %copy-done = f32[12,12,2048]{2,1,0:T(8,128)S(1)} copy-done((f32[12,12,2048]{2,1,0:T(8,128)S(1)}, f32[12,12,2048]{2,1,0:T(8,128)}, u32[]{:S(2)}) %copy-start) | copy-done | bytes 1179672
  2.0 0.0 copy-start.1
  2.0 1.0 %copy-done.1 = bf16[3,8,64,128]{3,2,1,0:T(8,128)(2,1)S(1)} copy-done((bf16[3,8,64,128]{3,2,1,0:T(8,128)(2,1)S(1)}, bf16[3,8,64,128]{3,2,1,0:T(8,128)(2,1)}, u32[]{:S(2)}) %copy-start.1) | copy-done | bytes 393240
  3.0 0.0 copy-start.2
  3.0 0.8 %copy-done.2 = f32[6,1024]{1,0:T(8,128)S(1)} copy-done((f32[6,1024]{1,0:T(8,128)S(1)}, f32[6,1024]{1,0:T(8,128)}, u32[]{:S(2)}) %copy-start.2) | copy-done | bytes 24600
  3.8 0.0 copy-start.3
  3.8 0.8 %copy-done.3 = f32[6,1024]{1,0:T(8,128)S(1)} copy-done((f32[6,1024]{1,0:T(8,128)S(1)}, f32[6,1024]{1,0:T(8,128)}, u32[]{:S(2)}) %copy-start.3) | copy-done | bytes 24600
  4.6 0.0 copy-start.4
  4.6 0.8 %copy-done.4 = f32[6,1024]{1,0:T(8,128)S(1)} copy-done((f32[6,1024]{1,0:T(8,128)S(1)}, f32[6,1024]{1,0:T(8,128)}, u32[]{:S(2)}) %copy-start.4) | copy-done | bytes 24600
  5.3 0.0 copy-start.5
  5.3 0.7 %copy-done.5 = s32[2,2048]{1,0:T(2,128)S(1)} copy-done((s32[2,2048]{1,0:T(2,128)S(1)}, s32[2,2048]{1,0:T(2,128)}, u32[]{:S(2)}) %copy-start.5) | copy-done | bytes 16408
  6.0 0.0 copy-start.6
  6.0 0.7 %copy-done.6 = f32[8,128]{1,0:T(8,128)S(1)} copy-done((f32[8,128]{1,0:T(8,128)S(1)}, f32[8,128]{1,0:T(8,128)}, u32[]{:S(2)}) %copy-start.6) | copy-done | bytes 4120
  6.7 0.0 copy-start.7
  6.7 0.7 %copy-done.7 = s32[8,128]{1,0:T(8,128)S(1)} copy-done((s32[8,128]{1,0:T(8,128)S(1)}, s32[8,128]{1,0:T(8,128)}, u32[]{:S(2)}) %copy-start.7) | copy-done | bytes 4120
  7.4 0.0 copy-start.8
  7.4 0.7 %copy-done.8 = s32[3,128]{1,0:T(4,128)S(1)} copy-done((s32[3,128]{1,0:T(4,128)S(1)}, s32[3,128]{1,0:T(4,128)}, u32[]{:S(2)}) %copy-start.8) | copy-done | bytes 1560
  8.1 0.0 copy-start.9
  8.1 0.7 %copy-done.9 = s32[8]{0:T(128)S(1)} copy-done((s32[8]{0:T(128)S(1)}, s32[8]{0:T(128)}, u32[]{:S(2)}) %copy-start.9) | copy-done | bytes 56
  8.7 49.9 %shard_map.138 = (f32[9,8,64,128]{3,2,1,0:T(8,128)S(1)}, f32[3,8,128]{2,1,0:T(8,128)S(1)}, f32[6,1024]{1,0:T(8,128)S(1)}, f32[6,1024]{1,0:T(8,128)S(1)}) custom-call(f32[9,8,64,128]{3,2,1,0:T(8,128)} %soil.1, bf16[3,8,64,128]{3,2,1,0:T(8,128)(2,1)S(1)} %copy-done.1, f32[8,128]{1,0:T(8,128)S(1)} %copy-done.6, s32[8,128]{1,0:T(8,128)S(1)} %copy-done.7, ...), custom_call_target="tpu_custom_call" | custom-call | tf_op jit(solution)/shard_map/pallas_call | solution.py:600
  58.7 1.4 %copy.19 = f32[9,8,64,128]{3,2,1,0:T(8,128)} copy(f32[9,8,64,128]{3,2,1,0:T(8,128)S(1)} %get-tuple-element.8) | data formatting | bytes 4718592
  60.1 0.6 copy.20
  60.7 0.6 copy.21
  61.3 0.6 copy.22
Async XLA Ops:
  0.6 1.4 %copy-start = (f32[12,12,2048]{2,1,0:T(8,128)S(1)}, f32[12,12,2048]{2,1,0:T(8,128)}, u32[]{:S(2)}) copy-start(f32[12,12,2048]{2,1,0:T(8,128)} %stiff.1) | copy-start | bytes 3538948
  2.0 1.0 %copy-start.1 = (bf16[3,8,64,128]{3,2,1,0:T(8,128)(2,1)S(1)}, bf16[3,8,64,128]{3,2,1,0:T(8,128)(2,1)}, u32[]{:S(2)}) copy-start(bf16[3,8,64,128]{3,2,1,0:T(8,128)(2,1)} %material.1) | copy-start | bytes 1179652
  3.0 0.8 %copy-start.2 = (f32[6,1024]{1,0:T(8,128)S(1)}, f32[6,1024]{1,0:T(8,128)}, u32[]{:S(2)}) copy-start(f32[6,1024]{1,0:T(8,128)} %inverse_mass.1) | copy-start | bytes 73732
  3.8 0.8 %copy-start.3 = (f32[6,1024]{1,0:T(8,128)S(1)}, f32[6,1024]{1,0:T(8,128)}, u32[]{:S(2)}) copy-start(f32[6,1024]{1,0:T(8,128)} %frame_disp.1) | copy-start | bytes 73732
  4.6 0.8 %copy-start.4 = (f32[6,1024]{1,0:T(8,128)S(1)}, f32[6,1024]{1,0:T(8,128)}, u32[]{:S(2)}) copy-start(f32[6,1024]{1,0:T(8,128)} %frame_vel.1) | copy-start | bytes 73732
  5.3 0.7 %copy-start.5 = (s32[2,2048]{1,0:T(2,128)S(1)}, s32[2,2048]{1,0:T(2,128)}, u32[]{:S(2)}) copy-start(s32[2,2048]{1,0:T(2,128)} %links.1) | copy-start | bytes 49156
  6.0 0.7 %copy-start.6 = (f32[8,128]{1,0:T(8,128)S(1)}, f32[8,128]{1,0:T(8,128)}, u32[]{:S(2)}) copy-start(f32[8,128]{1,0:T(8,128)} %dashpot.1) | copy-start | bytes 12292
  6.7 0.7 %copy-start.7 = (s32[8,128]{1,0:T(8,128)S(1)}, s32[8,128]{1,0:T(8,128)}, u32[]{:S(2)}) copy-start(s32[8,128]{1,0:T(8,128)} %foot.1) | copy-start | bytes 12292
  7.4 0.7 %copy-start.8 = (s32[3,128]{1,0:T(4,128)S(1)}, s32[3,128]{1,0:T(4,128)}, u32[]{:S(2)}) copy-start(s32[3,128]{1,0:T(4,128)} %table.1) | copy-start | bytes 4612
  8.1 0.7 %copy-start.9 = (s32[8]{0:T(128)S(1)}, s32[8]{0:T(128)}, u32[]{:S(2)}) copy-start(s32[8]{0:T(128)} %count.1) | copy-start | bytes 100
where the time goes:
time: 62.4 us; the launch traced here: 61.9 us
  Pallas kernels  49.9 us (80%)
  local copies, waits for them, and re-layouts  11.3 us (18%)
  between operations  0.66 us (1%)
    pallas_call x1, Pallas kernels, shards(): pl.pallas_call(functools.partial(kernel, n_gx, n_gy), out_shape=(jax.Shap...  49.9 us
    unnamed x24, local copies, waits for them, and re-layouts  11.3 us

commit v1 on v0

--- a/solution.py
+++ b/solution.py
@@ -55,16 +55,17 @@
     n_gy,
     soil,
     material,
-    dashpot,
-    foot,
-    table,
+    hbm_dashpot,
+    hbm_foot,
+    hbm_table,
     stiff,
-    links,
-    count,
-    inverse_mass,
-    frame_disp,
-    frame_vel,
-    soil_out,
+    hbm_links,
+    hbm_count,
+    hbm_inverse_mass,
+    hbm_frame_disp,
+    hbm_frame_vel,
+    moved_out,
+    str_b,
     force_out,
     disp_out,
     vel_out,
@@ -72,15 +73,23 @@
     vel_a,
     str_a,
     vel_b,
-    str_b,
     raw,
     coef,
     matrix,
+    dashpot,
+    foot,
+    table,
+    links,
+    count,
+    inverse_mass,
+    frame_disp,
+    frame_vel,
     spread,
-    pack_up,
-    pack_down,
+    band,
+    edges,
     from_low,
     from_high,
+    correction,
     owners,
     bids,
     damp_vec,
@@ -88,11 +97,11 @@
     vel,
     imass,
     foot_sum,
+    internal,
     index,
     row_buf,
     rows_all,
     load_sem,
-    store_sem,
     x_send,
     x_recv,
     y_send,
@@ -122,6 +131,21 @@
     load_stress = load(0, soil.at[pl.ds(SXX, 6)], first.at[pl.ds(SXX, 6), inner, rows])
     load_velocity = load(1, soil.at[pl.ds(0, 3)], first.at[pl.ds(0, 3), inner, rows])
     load_material = load(2, material, raw)
+    load_small = [
+        load(4 + k, source, target)
+        for k, (source, target) in enumerate(
+            (
+                (hbm_dashpot, dashpot),
+                (hbm_foot, foot),
+                (hbm_table, table),
+                (hbm_links, links),
+                (hbm_count, count),
+                (hbm_inverse_mass, inverse_mass),
+                (hbm_frame_disp, frame_disp),
+                (hbm_frame_vel, frame_vel),
+            )
+        )
+    ]
     load_matrix = load(3, stiff, matrix)
 
     barrier = pltpu.get_barrier_semaphore()
@@ -191,14 +215,14 @@
     def send_y(stage):
         return [
             remote(
-                pack_up.at[stage],
+                edges.at[stage],
                 from_low.at[stage],
                 y_send.at[stage, 0],
                 y_recv.at[stage, 0],
                 {"gy": gy_up},
             ),
             remote(
-                pack_down.at[stage],
+                edges.at[stage],
                 from_high.at[stage],
                 y_send.at[stage, 1],
                 y_recv.at[stage, 1],
@@ -206,9 +230,12 @@
             ),
         ]
 
+    leaving = []
+
     def finish(copies):
         for copy in copies:
-            copy.wait()
+            copy.wait_recv()
+        leaving.extend(copies)
 
     def outside_zero_x(ref, members, low, high):
         @pl.when(gx == 0)
@@ -223,54 +250,75 @@
                 for layer in range(high):
                     ref[member, COL + cells_x + layer, rows, :] = jnp.zeros((cells_z, cells_y), F32)
 
-    def outside_zero_y(stage):
-        @pl.when(gy == 0)
-        def _():
-            from_low[stage] = jnp.zeros(from_low.shape[1:], F32)
-
-        @pl.when(gy == n_gy - 1)
-        def _():
-            from_high[stage] = jnp.zeros(from_high.shape[1:], F32)
-
     lane = iota((8, cells_y), 1)
-    lane_single, lane_double = lane, lane // 2
-
-    def pack(packed, values, tile, up):
-        ups, downs = packed
-        if up == 2:
-            up_mask, down_mask = lane_double == tile, lane_single == tile
-            up_shift, down_shift = lax.rem(2 * tile + 2, 128), tile
-        else:
-            up_mask, down_mask = lane_single == tile, lane_double == tile
-            up_shift, down_shift = tile + 1, 2 * tile
-        ups = tuple(
-            jnp.where(up_mask, rolled(value, up_shift), old) for value, old in zip(values, ups)
-        )
-        downs = tuple(
-            jnp.where(down_mask, rolled(value, down_shift), old) for value, old in zip(values, downs)
-        )
-        return ups, downs
-
-    nothing = (tuple([zero_tile] * 3), tuple([zero_tile] * 3))
-
-    def keep_packed(stage, packed):
+    slot = lane & 3
+
+    def pack(stage, values, cell):
+        group = cell // 4
         for k in range(3):
-            pack_up[stage, k] = packed[0][k]
-            pack_down[stage, k] = packed[1][k]
-
-    def along_y(value, stage, k, tile, forward):
-        if forward:
-            low = jnp.where(
-                lane == cells_y - 1, rolled(from_low[stage, k], lax.rem(127 - tile, 128)), value
-            )
-            beyond = rolled(from_high[stage, k], lax.rem(128 - 2 * tile, 128))
-            near, far = jnp.where(lane < 1, beyond, value), jnp.where(lane < 2, beyond, value)
-            return stencil(rolled(near, 127), value, rolled(far, 126), rolled(low, 1))
-        beyond = rolled(from_low[stage, k], lax.rem(254 - 2 * tile, 128))
-        near = jnp.where(lane == cells_y - 1, beyond, value)
-        far = jnp.where(lane >= cells_y - 2, beyond, value)
-        high = jnp.where(lane < 1, rolled(from_high[stage, k], lax.rem(128 - tile, 128)), value)
-        return stencil(value, rolled(near, 1), rolled(high, 127), rolled(far, 2))
+            packed = edges[stage, k, group]
+            for z in range(tiles_z):
+                place = (cell & 3) * tiles_z + z
+                packed = jnp.where(
+                    lane >> 2 == place, rolled(values[z][k], (4 * place + 2) & 127), packed
+                )
+            edges[stage, k, group] = packed
+
+    def prepare(stage, forward):
+        for k in range(3):
+            for group in range(edges.shape[2]):
+                low = jnp.where(gy > 0, from_low[stage, k, group], 0.0)
+                high = jnp.where(gy < n_gy - 1, from_high[stage, k, group], 0.0)
+                beyond = jnp.where(slot < 2, low, high)
+                back_2, back_1 = rolled(beyond, 126), rolled(beyond, 127)
+                on_1, on_2 = rolled(beyond, 1), rolled(beyond, 2)
+                if forward:
+                    value = jnp.where(
+                        slot == 0,
+                        FAR * back_2,
+                        jnp.where(
+                            slot == 1,
+                            NEAR * back_1 + FAR * back_2,
+                            jnp.where(slot == 2, -FAR * on_1, 0.0),
+                        ),
+                    )
+                else:
+                    value = jnp.where(
+                        slot == 1,
+                        FAR * back_1,
+                        jnp.where(
+                            slot == 2,
+                            -NEAR * on_1 - FAR * on_2,
+                            jnp.where(slot == 3, -FAR * on_2, 0.0),
+                        ),
+                    )
+                correction[stage, k, group] = value
+
+    at_edge = (lane < 2) | (lane >= cells_y - 2)
+
+    def along_y(ref, members, stage, cell, forward):
+        parts = []
+        for member in members:
+            value = ref[member, cell + COL, rows, :]
+            high = value.astype(BF16)
+            low = (value - high.astype(F32)).astype(BF16)
+            parts.append(jnp.concatenate([high, low], 1))
+        both = jnp.dot(
+            jnp.concatenate(parts, 0), band[int(forward)], preferred_element_type=F32
+        )
+        group = cell // 4
+        result = []
+        for z in range(tiles_z):
+            shift = (254 - 4 * ((cell & 3) * tiles_z + z)) & 127
+            line = []
+            for k in range(3):
+                tile = slice(k * cells_z + 8 * z, k * cells_z + 8 * z + 8)
+                inside = NEAR * both[tile, 0:128] + FAR * both[tile, 128:256]
+                line.append(
+                    inside + jnp.where(at_edge, rolled(correction[stage, k, group], shift), 0.0)
+                )
+            result.append(line)
+        return result
 
     def at(ref, member, x, row):
         return ref[member, x, pl.ds(row, 8), :]
@@ -293,19 +341,17 @@
             at(ref, member, x, row + shift - 2),
         )
 
-    def velocity_layers(stage, stress, base, old, new, begin, end, packed):
+    def velocity_layers(stage, stress, base, old, new, begin, end, out=None):
         sxx, syy, szz, sxy, sxz, syz = range(base, base + 6)
 
-        def layer(i, packed):
-            cell = lax.rem(i + cells_x - 1, cells_x)
+        def layer(i, carry):
+            cell = (i + cells_x - 1) & (cells_x - 1)
             x = cell + COL
+            y_all = along_y(stress, (sxy, syy, syz), stage, cell, False)
+            results = []
             for z in range(tiles_z):
                 row = ROW + 8 * z
-                tile = cell * tiles_z + z
-                y_of = [
-                    along_y(at(stress, member, x, row), stage, k, tile, False)
-                    for k, member in enumerate((sxy, syy, syz))
-                ]
+                y_of = y_all[z]
                 accel = (
                     along_x(stress, sxx, x, row, False) + y_of[0] + along_z(stress, sxz, x, row, False),
                     along_x(stress, sxy, x, row, False) + y_of[1] + along_z(stress, syz, x, row, False),
@@ -315,21 +361,23 @@
                 after = [at(old, k, x, row) + density * accel[k] for k in range(3)]
                 for k in range(3):
                     new[k, x, pl.ds(row, 8), :] = after[k]
-                packed = pack(packed, after, tile, 1)
-            return packed
-
-        return lax.fori_loop(begin, end, layer, packed)
-
-    def stress_layers(stage, moving, stress, base, new, new_x, new_row, begin, end, packed):
-        def layer(i, packed):
-            cell = lax.rem(i + cells_x - 2, cells_x)
+                    if out is not None:
+                        out[k, cell, pl.ds(8 * z, 8), :] = after[k]
+                results.append(after)
+            pack(stage + 1, results, cell)
+            return carry
+
+        lax.fori_loop(begin, end, layer, 0)
+
+    def stress_layers(stage, moving, stress, base, new, new_x, new_row, begin, end, packing):
+        def layer(i, carry):
+            cell = (i + cells_x - 2) & (cells_x - 1)
             x = cell + COL
+            y_all = along_y(moving, (0, 1, 2), stage, cell, True)
+            results = []
             for z in range(tiles_z):
                 row = ROW + 8 * z
-                tile = cell * tiles_z + z
-                y_of = [
-                    along_y(at(moving, k, x, row), stage, k, tile, True) for k in range(3)
-                ]
+                y_of = y_all[z]
                 x_of = [along_x(moving, k, x, row, True) for k in range(3)]
                 z_of = [along_z(moving, k, x, row, True) for k in range(3)]
                 lame = coef[1, cell, pl.ds(8 * z, 8), :]
@@ -347,19 +395,12 @@
                 after = [at(stress, base + k, x, row) + change[k] for k in range(6)]
                 for k in range(6):
                     new[k, cell + new_x, pl.ds(new_row + 8 * z, 8), :] = after[k]
-                if packed is not None:
-                    packed = pack(packed, (after[3], after[1], after[5]), tile, 2)
-            return packed
-
-        if packed is None:
-
-            def bare(i, carry):
-                layer(i, None)
-                return carry
-
-            lax.fori_loop(begin, end, bare, 0)
-            return None
-        return lax.fori_loop(begin, end, layer, packed)
+                results.append((after[3], after[1], after[5]))
+            if packing:
+                pack(stage + 1, results, cell)
+            return carry
+
+        lax.fori_loop(begin, end, layer, 0)
 
     stress_groups = ((SXX, SXX, 1), (SXY, SXY, 2))
     inner_groups = ((0, 0, 1), (3, 3, 2))
@@ -368,14 +409,26 @@
     sent = send_x(0, soil, 0, first, stress_groups, 2, 1)
     load_stress.wait()
 
-    def pack_first(cell, packed):
-        for z in range(tiles_z):
-            values = [at(first, k, cell + COL, ROW + 8 * z) for k in (SXY, SYY, SYZ)]
-            packed = pack(packed, values, cell * tiles_z + z, 2)
-        return packed
-
-    keep_packed(0, lax.fori_loop(0, cells_x, pack_first, nothing))
+    edges[...] = jnp.zeros(edges.shape, F32)
+
+    def pack_first(cell, carry):
+        values = [
+            [at(first, k, cell + COL, ROW + 8 * z) for k in (SXY, SYY, SYZ)] for z in range(tiles_z)
+        ]
+        pack(0, values, cell)
+        return carry
+
+    lax.fori_loop(0, cells_x, pack_first, 0)
     sent += send_y(0)
+
+    source = iota((256, 256), 0) & 127
+    column = iota((256, 256), 1)
+    wanted = column & 127
+    for forward in range(2):
+        reach = jnp.where(column < 128, 0, 1)
+        plus = source == wanted + forward + reach
+        minus = source == wanted + forward - 1 - reach
+        band[forward] = jnp.where(plus, 1.0, jnp.where(minus, -1.0, 0.0)).astype(BF16)
 
     load_material.wait()
 
@@ -389,14 +442,15 @@
 
     finish(sent)
     outside_zero_x(first, (SXX, SXY, SXZ), 2, 1)
-    outside_zero_y(0)
-
-    packed = velocity_layers(0, first, SXX, first, vel_a, 0, 3, nothing)
+    prepare(0, False)
+
+    velocity_layers(0, first, SXX, first, vel_a, 0, 3)
     sent = send_x(1, vel_a, COL, vel_a, move_groups, 1, 2)
-    packed = velocity_layers(0, first, SXX, first, vel_a, 3, cells_x, packed)
-    keep_packed(1, packed)
+    velocity_layers(0, first, SXX, first, vel_a, 3, cells_x)
     sent += send_y(1)
 
+    for copy in load_small:
+        copy.wait()
     big = (128, 128)
     big_lane = iota(big, 1)
     big_lane_f = big_lane.astype(F32)
@@ -442,29 +496,59 @@
         imass[b] = TIME_FRAME * jnp.concatenate([inverse_mass[:, piece], blank], 0)
         foot_sum[b] = jnp.zeros((8, 128), F32)
 
+    load_matrix.wait()
+
+    def internal_forces(b):
+        place = disp[b]
+        forces = []
+        for h in range(2):
+            ends = (
+                lane_gather(place, index[b, h * 2]),
+                lane_gather(place, index[b, h * 2 + 1]),
+            )
+            piece = pl.ds(b * 256 + h * 128, 128)
+            total = None
+            for a in range(12):
+                row = ends[a // 6][a % 6 : a % 6 + 1, :]
+                term = matrix[a, :, piece] * row
+                total = term if total is None else total + term
+            forces.append(jnp.concatenate([total, jnp.zeros((4, 128), F32)], 0))
+        forces = jnp.concatenate(forces, 1)
+        high = forces.astype(BF16)
+        low = (forces - high.astype(F32)).astype(BF16)
+        parts = jnp.dot(
+            jnp.concatenate([high, low], 0), spread[b], preferred_element_type=F32
+        )
+        parts = parts[0:16] + parts[16:32]
+        internal[b] = parts[0:8, 0:128] + parts[6:14, 128:256]
+
+    def advance(b):
+        speed = vel[b]
+        loads = damp_vec[0, b] - damp_vec[1, b] * speed - internal[b]
+        speed = speed + imass[b] * loads
+        vel[b] = speed
+        disp[b] = disp[b] + TIME_FRAME * speed
+        foot_sum[b] += speed
+
+    for b in range(buildings):
+        internal_forces(b)
+
     finish(sent)
     outside_zero_x(vel_a, (0, 1, 2), 1, 2)
-    outside_zero_y(1)
-
-    packed = stress_layers(1, vel_a, first, SXX, str_a, COL, ROW, 0, 3, nothing)
+    prepare(1, True)
+
+    stress_layers(1, vel_a, first, SXX, str_a, COL, ROW, 0, 3, True)
     sent = send_x(2, str_a, COL, str_a, inner_groups, 2, 1)
-    packed = stress_layers(1, vel_a, first, SXX, str_a, COL, ROW, 3, cells_x, packed)
-    keep_packed(2, packed)
+    stress_layers(1, vel_a, first, SXX, str_a, COL, ROW, 3, cells_x, True)
     sent += send_y(2)
     finish(sent)
     outside_zero_x(str_a, (0, 3, 4), 2, 1)
-    outside_zero_y(2)
-
-    packed = velocity_layers(2, str_a, 0, vel_a, vel_b, 0, 3, nothing)
-    sent = send_x(3, vel_b, COL, vel_b, move_groups, 1, 2)
-    packed = velocity_layers(2, str_a, 0, vel_a, vel_b, 3, cells_x, packed)
-    keep_packed(3, packed)
-    sent += send_y(3)
-
-    store_velocity = pltpu.make_async_copy(
-        vel_b.at[:, inner, rows], soil_out.at[pl.ds(0, 3)], store_sem.at[0]
-    )
-    store_velocity.start()
+    prepare(2, False)
+
+    velocity_layers(2, str_a, 0, vel_a, vel_b, 0, 3, moved_out)
+    sent_x = send_x(3, vel_b, COL, vel_b, move_groups, 1, 2)
+    velocity_layers(2, str_a, 0, vel_a, vel_b, 3, cells_x, moved_out)
+    sent_y = send_y(3)
 
     surface = [vel_b[k, inner, ROW, :] for k in range(3)]
     dash = dashpot[...]
@@ -478,9 +562,9 @@
     sums = jnp.concatenate(sums + [jnp.zeros((128 - len(sums), 128), F32)], 0)
     mine = jnp.sum(sums.T, axis=0, keepdims=True)
 
-    def gather_rows(turn, value):
+    def gather_along_gy(turn, value):
         row_buf[turn, gy] = value
-        sent = [
+        return [
             remote(
                 row_buf.at[turn, gy],
                 row_buf.at[turn, gy],
@@ -490,7 +574,8 @@
             )
             for k in range(1, n_gy)
         ]
-        finish(sent)
+
+    def gather_along_gx(turn):
         rows_all[turn, gx] = row_buf[turn].reshape(n_gy, 128)
         return [
             remote(
@@ -503,22 +588,22 @@
             for k in range(1, n_gx)
         ]
 
-    gathering = gather_rows(0, mine)
-
-    finish(sent)
+    gathering = gather_along_gy(0, mine)
+
+    finish(sent_y)
+    prepare(3, True)
+    stress_layers(3, vel_b, str_a, 0, str_b, 0, 0, 3, cells_x, False)
+    finish(gathering)
+    gathering = gather_along_gx(0)
+    finish(sent_x)
     outside_zero_x(vel_b, (0, 1, 2), 1, 2)
-    outside_zero_y(3)
-    stress_layers(3, vel_b, str_a, 0, str_b, 0, 0, 0, cells_x, None)
-    store_stress = pltpu.make_async_copy(str_b, soil_out.at[pl.ds(3, 6)], store_sem.at[1])
-    store_stress.start()
-
+    stress_layers(3, vel_b, str_a, 0, str_b, 0, 0, 0, 3, False)
     finish(gathering)
     arrived = rows_all[0].reshape(n_dev, 128)
     owned = jnp.sum(jnp.where(owners[...] == me, arrived, 0.0), axis=0, keepdims=True)
     owned = jnp.broadcast_to(owned, (8, 128))
 
     at_footing = (small_row < 3) & (small_lane == 0)
-    load_matrix.wait()
     drives, dampers = [], []
     for b in range(buildings):
         pick = jnp.minimum(small_row * buildings + b, 127)
@@ -531,49 +616,27 @@
 
     def frame_step(step, carry):
         for b in range(buildings):
-            place = disp[b]
-            forces = []
-            for h in range(2):
-                ends = (
-                    lane_gather(place, index[b, h * 2]),
-                    lane_gather(place, index[b, h * 2 + 1]),
-                )
-                piece = pl.ds(b * 256 + h * 128, 128)
-                total = None
-                for a in range(12):
-                    row = ends[a // 6][a % 6 : a % 6 + 1, :]
-                    term = matrix[a, :, piece] * row
-                    total = term if total is None else total + term
-                forces.append(jnp.concatenate([total, jnp.zeros((4, 128), F32)], 0))
-            forces = jnp.concatenate(forces, 1)
-            high = forces.astype(BF16)
-            low = (forces - high.astype(F32)).astype(BF16)
-            parts = jnp.dot(
-                jnp.concatenate([high, low], 0), spread[b], preferred_element_type=F32
-            )
-            parts = parts[0:16] + parts[16:32]
-            internal = parts[0:8, 0:128] + parts[6:14, 128:256]
-            speed = vel[b]
-            loads = damp_vec[0, b] - damp_vec[1, b] * speed - internal
-            speed = speed + imass[b] * loads
-            vel[b] = speed
-            disp[b] = place + TIME_FRAME * speed
-            foot_sum[b] += speed
+            advance(b)
+            internal_forces(b)
         return carry
 
-    lax.fori_loop(0, FRAME_STEPS, frame_step, 0)
+    lax.fori_loop(0, FRAME_STEPS - 1, frame_step, 0)
+    for b in range(buildings):
+        advance(b)
 
     back = jnp.zeros((8, 128), F32)
     for b in range(buildings):
         whole = jnp.broadcast_to(foot_sum[b][:, 0:1], (8, 128))
         back = jnp.where(small_lane == small_row * buildings + b, whole, back)
     back = jnp.where(small_row < 3, back, 0.0)
-    gathering = gather_rows(1, jnp.sum(back, axis=0, keepdims=True))
+    gathering = gather_along_gy(1, jnp.sum(back, axis=0, keepdims=True))
     for b in range(buildings):
         piece = pl.ds(b * 128, 128)
         disp_out[:, piece] = disp[b][0:6]
         vel_out[:, piece] = vel[b][0:6]
     wanted = owners[pl.ds(me, 1), :]
+    finish(gathering)
+    gathering = gather_along_gx(1)
     finish(gathering)
     arrived = rows_all[1].reshape(n_dev, 128)
     held = jnp.where(iota((n_dev, 128), 0) == wanted, arrived, 0.0)
@@ -582,9 +645,27 @@
         total = lane_gather(held, bid + k * buildings)
         force_out[k] = dash * (FRAME_STEPS * surface[k] - total)
 
-    finish(sent[:0])
-    store_velocity.wait()
-    store_stress.wait()
+    for copy in leaving:
+        copy.wait_send()
+
+
+def write_out(moved, stress, force, disp, vel, soil_out, force_out, disp_out, vel_out, sem):
+    copies = [
+        pltpu.make_async_copy(source, target, sem.at[k])
+        for k, (source, target) in enumerate(
+            (
+                (stress, soil_out.at[pl.ds(3, 6)]),
+                (moved, soil_out.at[pl.ds(0, 3)]),
+                (force, force_out),
+                (disp, disp_out),
+                (vel, vel_out),
+            )
+        )
+    ]
+    for copy in copies:
+        copy.start()
+    for copy in copies:
+        copy.wait()
 
 
 def shards(n_gx, n_gy, *args):
@@ -595,32 +676,42 @@
     n_dev = n_gx * n_gy
     anywhere = pl.BlockSpec(memory_space=pl.ANY)
     vmem = pl.BlockSpec(memory_space=pltpu.VMEM)
-    smem = pl.BlockSpec(memory_space=pltpu.SMEM)
     dma = pltpu.SemaphoreType.DMA
-    return pl.pallas_call(
+    limit = 40 * 1024 * 1024
+    kept = (
+        pltpu.VMEM((3, cells_x, cells_z, cells_y), F32),
+        pltpu.VMEM((6, cells_x, cells_z, cells_y), F32),
+        pltpu.VMEM((3, cells_x, cells_y), F32),
+        pltpu.VMEM(args[9].shape, F32),
+        pltpu.VMEM(args[10].shape, F32),
+    )
+    results = pl.pallas_call(
         functools.partial(kernel, n_gx, n_gy),
-        out_shape=(
-            jax.ShapeDtypeStruct(soil.shape, F32),
-            jax.ShapeDtypeStruct((3, cells_x, cells_y), F32),
-            jax.ShapeDtypeStruct(args[9].shape, F32),
-            jax.ShapeDtypeStruct(args[10].shape, F32),
-        ),
-        in_specs=[anywhere, anywhere, vmem, vmem, vmem, anywhere, vmem, smem, vmem, vmem, vmem],
-        out_specs=(anywhere, vmem, vmem, vmem),
+        out_shape=kept,
+        in_specs=[pl.BlockSpec(memory_space=pltpu.HBM)] * len(args),
+        out_specs=(vmem,) * len(kept),
         scratch_shapes=[
             pltpu.VMEM((9,) + wide, F32),
             pltpu.VMEM((3,) + wide, F32),
             pltpu.VMEM((6,) + wide, F32),
             pltpu.VMEM((3,) + wide, F32),
-            pltpu.VMEM((6, cells_x, cells_z, cells_y), F32),
             pltpu.VMEM(material.shape, BF16),
             pltpu.VMEM(material.shape, F32),
             pltpu.VMEM(stiff.shape, F32),
+            pltpu.VMEM(dashpot.shape, F32),
+            pltpu.VMEM(foot.shape, jnp.int32),
+            pltpu.VMEM(table.shape, jnp.int32),
+            pltpu.VMEM(links.shape, jnp.int32),
+            pltpu.SMEM(args[7].shape, jnp.int32),
+            pltpu.VMEM(args[8].shape, F32),
+            pltpu.VMEM(args[9].shape, F32),
+            pltpu.VMEM(args[10].shape, F32),
             pltpu.VMEM((buildings, 256, 256), BF16),
-            pltpu.VMEM((4, 3, 8, 128), F32),
-            pltpu.VMEM((4, 3, 8, 128), F32),
-            pltpu.VMEM((4, 3, 8, 128), F32),
-            pltpu.VMEM((4, 3, 8, 128), F32),
+            pltpu.VMEM((2, 256, 256), BF16),
+            pltpu.VMEM((4, 3, cells_x // 4, 8, 128), F32),
+            pltpu.VMEM((4, 3, cells_x // 4, 8, 128), F32),
+            pltpu.VMEM((4, 3, cells_x // 4, 8, 128), F32),
+            pltpu.VMEM((4, 3, cells_x // 4, 8, 128), F32),
             pltpu.VMEM((n_dev, 128), jnp.int32),
             pltpu.VMEM((8, 128), jnp.int32),
             pltpu.VMEM((2, buildings, 8, 128), F32),
@@ -628,11 +719,11 @@
             pltpu.VMEM((buildings, 8, 128), F32),
             pltpu.VMEM((buildings, 8, 128), F32),
             pltpu.VMEM((buildings, 8, 128), F32),
+            pltpu.VMEM((buildings, 8, 128), F32),
             pltpu.VMEM((buildings, 4, 8, 128), jnp.int32),
             pltpu.VMEM((2, n_gy, 1, 128), F32),
             pltpu.VMEM((2, n_gx, n_gy, 128), F32),
-            dma((4,)),
-            dma((2,)),
+            dma((12,)),
             dma((4, 2, 2)),
             dma((4, 2, 2)),
             dma((4, 2)),
@@ -643,9 +734,22 @@
             dma((2, n_gx - 1)),
         ],
         compiler_params=pltpu.CompilerParams(
-            collective_id=0, has_side_effects=True, vmem_limit_bytes=48 * 1024 * 1024
+            collective_id=0, has_side_effects=True, vmem_limit_bytes=limit
         ),
-    )(*args)
+    )(*(pltpu.with_memory_space_constraint(value, pltpu.HBM) for value in args))
+    return pl.pallas_call(
+        write_out,
+        out_shape=(
+            jax.ShapeDtypeStruct(soil.shape, F32),
+            jax.ShapeDtypeStruct((3, cells_x, cells_y), F32),
+            jax.ShapeDtypeStruct(args[9].shape, F32),
+            jax.ShapeDtypeStruct(args[10].shape, F32),
+        ),
+        in_specs=[vmem] * len(kept),
+        out_specs=(anywhere,) * 4,
+        scratch_shapes=[dma((len(kept),))],
+        compiler_params=pltpu.CompilerParams(vmem_limit_bytes=limit),
+    )(*results)
 
 
 def solution(mesh):

time: 62.4 us -> 51.5 us (0.83)
  local copies, waits for them, and re-layouts: 11.3 us -> 0 us
  Pallas kernels: 49.9 us -> 50.7 us
    unnamed x24 -> x0, local copies, waits for them, and re-layouts: 11.3 us -> none
    pallas_call x1 -> x2, Pallas kernels: 49.9 us -> 50.7 us  [the longest x1 49.3 us: shards(): pl.pallas_call(functools.partial(kernel, n_gx, n_gy), out_shape=kept, in_...]
where the time goes in v1:
time: 51.5 us; the launch traced here: 51.4 us
  Pallas kernels  50.7 us (98%)
  between operations  0.64 us (1%)
    pallas_call x1, Pallas kernels, shards(): pl.pallas_call(functools.partial(kernel, n_gx, n_gy), out_shape=kept, in_...  49.3 us
    pallas_call x1, Pallas kernels, shards(): pl.pallas_call(write_out, out_shape=(jax.ShapeDtypeStruct(soil.shape, F32...  1.45 us

profile of v1, /device:TPU:1, one launch (start us, length us, event | category | flops | bytes accessed | tf_op | source)
XLA Modules:
  0.0 51.4 jit_solution(2090713384828799546)
XLA Ops:
  0.6 49.3 %shard_map.138 = (f32[3,8,64,128]{3,2,1,0:T(8,128)S(1)}, f32[6,8,64,128]{3,2,1,0:T(8,128)S(1)}, f32[3,8,128]{2,1,0:T(8,128)S(1)}, f32[6,1024]{1,0:T(8,128)S(1)}, f32[6,1024]{1,0:T(8,128)S(1)}) custom-call(f32[9,8,64,128]{3,2,1,0:T(8,128)} %soil.1, bf16[3,8,64,128]{3,2,1,0:T(8,128)(2,1)} %material.1, f32[8,128]{1,0:T(8,128)} %hbm_dashpot.1, ...), custom_call_target="tpu_custom_call" | custom-call | tf_op jit(solution)/shard_map/pallas_call | solution.py:688
  49.9 1.5 %shard_map.139 = (f32[9,8,64,128]{3,2,1,0:T(8,128)}, f32[3,8,128]{2,1,0:T(8,128)}, f32[6,1024]{1,0:T(8,128)}, f32[6,1024]{1,0:T(8,128)}) custom-call(f32[3,8,64,128]{3,2,1,0:T(8,128)S(1)} %get-tuple-element.9.moved, f32[6,8,64,128]{3,2,1,0:T(8,128)S(1)} %get-tuple-element.10.stress, f32[3,8,128]{2,1,0:T(8,128)S(1)} %get-tuple-element.11.force, ...), custom_call_target="tpu_custom_call" | custom-call | tf_op jit(solution)/shard_map/pallas_call | solution.py:740

commit v2 on v1

--- a/solution.py
+++ b/solution.py
@@ -16,6 +16,7 @@
 MESH = pl.DeviceIdType.MESH
 ROW = 8
 COL = 2
+LOW, HIGH = 5, 4
 F32 = jnp.float32
 BF16 = jnp.bfloat16
 
@@ -90,6 +91,9 @@
     from_low,
     from_high,
     correction,
+    top,
+    rims,
+    rims_in,
     owners,
     bids,
     damp_vec,
@@ -110,6 +114,8 @@
     a_recv,
     b_send,
     b_recv,
+    t_send,
+    t_recv,
 ):
     gx = lax.axis_index("gx")
     gy = lax.axis_index("gy")
@@ -158,6 +164,12 @@
             barrier, inc=1, device_id={"gy": lax.rem(gy + k, n_gy)}, device_id_type=MESH
         )
 
+    corners = [
+        {"gx": row, "gy": column} for row in (gx_down, gx_up) for column in (gy_down, gy_up)
+    ]
+    for device in corners:
+        pl.semaphore_signal(barrier, inc=1, device_id=device, device_id_type=MESH)
+
     zero_tile = jnp.zeros((8, cells_y), F32)
 
     def clear(x, carry):
@@ -174,7 +186,13 @@
 
     lax.fori_loop(COL, COL + cells_x, clear, 0)
 
-    pl.semaphore_wait(barrier, n_gx + n_gy - 2)
+    def clear_top(x, carry):
+        for member in (VX, VY, VZ, SZZ, SXZ, SYZ):
+            for part in range(2):
+                top[member, x, part, pl.ds(0, 8), :] = zero_tile
+        return carry
+
+    lax.fori_loop(0, top.shape[1], clear_top, 0)
 
     def remote(source, target, send, recv, device):
         copy = pltpu.make_async_remote_copy(
@@ -406,7 +424,190 @@
     inner_groups = ((0, 0, 1), (3, 3, 2))
     move_groups = ((0, 0, 3),)
 
-    sent = send_x(0, soil, 0, first, stress_groups, 2, 1)
+    fields = rims.shape[0]
+    wide_lane = lane
+
+    def pack_rims(cell, carry):
+        for member in range(fields):
+            if member < 9:
+                value = at(first, member, cell + COL, ROW)
+            else:
+                value = coef[member - 9, cell, pl.ds(0, 8), :]
+            top[member, cell + LOW, 0, pl.ds(8, 8), :] = value
+            rims[member] = jnp.where(
+                wide_lane >> 4 == cell, rolled(value, (16 * cell + LOW) & 127), rims[member]
+            )
+        return carry
+
+    def send_top():
+        copies = []
+        top_rows = pl.ds(8, 8)
+        flow = (
+            (first, VX, 3, VX, 3, 3, ROW, COL),
+            (first, SXX, 6, SXX, LOW, HIGH, ROW, COL),
+            (coef, 0, 3, 9, 3, 3, 0, 0),
+        )
+        for k, (source, origin, size, member, up, down, row, layer) in enumerate(flow):
+            copies.append(
+                remote(
+                    source.at[pl.ds(origin, size), pl.ds(layer + cells_x - up, up), pl.ds(row, 8)],
+                    top.at[pl.ds(member, size), pl.ds(LOW - up, up), 0, top_rows],
+                    t_send.at[k],
+                    t_recv.at[k],
+                    {"gx": gx_up},
+                )
+            )
+            copies.append(
+                remote(
+                    source.at[pl.ds(origin, size), pl.ds(layer, down), pl.ds(row, 8)],
+                    top.at[pl.ds(member, size), pl.ds(LOW + cells_x, down), 0, top_rows],
+                    t_send.at[3 + k],
+                    t_recv.at[3 + k],
+                    {"gx": gx_down},
+                )
+            )
+        for k, (device, row, column, size) in enumerate(
+            (
+                ({"gx": gx_up, "gy": gy_up}, 0, 0, fields - 2),
+                ({"gx": gx_up, "gy": gy_down}, 0, 1, fields - 2),
+                ({"gx": gx_down, "gy": gy_up}, 2, 0, fields - 2),
+                ({"gx": gx_down, "gy": gy_down}, 2, 1, fields - 2),
+                ({"gy": gy_up}, 1, 0, fields),
+                ({"gy": gy_down}, 1, 1, fields),
+            )
+        ):
+            copies.append(
+                remote(
+                    rims.at[pl.ds(0, size)],
+                    rims_in.at[row, column, pl.ds(0, size)],
+                    t_send.at[6 + k],
+                    t_recv.at[6 + k],
+                    device,
+                )
+            )
+        return copies
+
+    def unpack_rims():
+        spot = wide_lane & 15
+
+        def fill(row, member, shown, x, cell):
+            low = jnp.where(shown & (gy > 0), rims_in[row, 0, member], 0.0)
+            high = jnp.where(shown & (gy < n_gy - 1), rims_in[row, 1, member], 0.0)
+            both = jnp.where(spot < LOW, low, high)
+            both = rolled(both, (256 - LOW - 16 * cell) & 127)
+            near = (wide_lane < HIGH) | (wide_lane >= 128 - LOW)
+            top[member, x, 1, pl.ds(8, 8), :] = jnp.where(near, both, 0.0)
+
+        def layer_inside(cell, carry):
+            for member in range(fields):
+                fill(1, member, True, cell + LOW, cell)
+            return carry
+
+        lax.fori_loop(0, cells_x, layer_inside, 0)
+
+        def layer_low(x, carry):
+            for member in range(fields - 2):
+                fill(0, member, gx > 0, x, x + cells_x - LOW)
+            for member in range(fields - 2, fields):
+                top[member, x, 1, pl.ds(8, 8), :] = zero_tile
+            return carry
+
+        lax.fori_loop(0, LOW, layer_low, 0)
+
+        def layer_high(cell, carry):
+            for member in range(fields - 2):
+                fill(2, member, gx < n_gx - 1, cell + LOW + cells_x, cell)
+            for member in range(fields - 2, fields):
+                top[member, cell + LOW + cells_x, 1, pl.ds(8, 8), :] = zero_tile
+            return carry
+
+        lax.fori_loop(0, HIGH, layer_high, 0)
+
+        def outside(x, carry):
+            for member in range(fields):
+                top[member, x, 0, pl.ds(8, 8), :] = zero_tile
+            return carry
+
+        @pl.when(gx == 0)
+        def _():
+            lax.fori_loop(0, LOW, outside, 0)
+
+        @pl.when(gx == n_gx - 1)
+        def _():
+            lax.fori_loop(LOW + cells_x, LOW + cells_x + HIGH, outside, 0)
+
+    def top_at(member, x, part, row=8):
+        return top[member, x, part, pl.ds(row, 8), :]
+
+    def top_along_y(member, x, forward):
+        parts = [top_at(member, x, 0), top_at(member, x, 1)]
+
+        def moved(shift):
+            mine, other = [rolled(part, shift & 127) for part in parts]
+            across = wide_lane < shift if shift > 0 else wide_lane >= 128 + shift
+            return jnp.where(across, other, mine), jnp.where(across, mine, other)
+
+        if forward:
+            terms = (moved(-1), parts, moved(-2), moved(1))
+        else:
+            terms = (parts, moved(1), moved(-1), moved(2))
+        return [stencil(*(term[part] for term in terms)) for part in range(2)]
+
+    def top_along_x(member, x, part, shift):
+        return stencil(
+            top_at(member, x + shift, part),
+            top_at(member, x + shift - 1, part),
+            top_at(member, x + shift + 1, part),
+            top_at(member, x + shift - 2, part),
+        )
+
+    def top_along_z(member, x, part, shift):
+        return stencil(
+            top_at(member, x, part, 8 + shift),
+            top_at(member, x, part, 7 + shift),
+            top_at(member, x, part, 9 + shift),
+            top_at(member, x, part, 6 + shift),
+        )
+
+    def top_velocity(x, parts):
+        y_of = [top_along_y(member, x, False) for member in (SXY, SYY, SYZ)]
+        for part in range(parts):
+            accel = (
+                top_along_x(SXX, x, part, 0) + y_of[0][part] + top_along_z(SXZ, x, part, 0),
+                top_along_x(SXY, x, part, 0) + y_of[1][part] + top_along_z(SYZ, x, part, 0),
+                top_along_x(SXZ, x, part, 0) + y_of[2][part] + top_along_z(SZZ, x, part, 0),
+            )
+            for k in range(3):
+                top[k, x, part, pl.ds(8, 8), :] = (
+                    top_at(k, x, part) + top_at(9, x, part) * accel[k]
+                )
+
+    def top_stress(x):
+        y_of = [top_along_y(member, x, True) for member in range(3)]
+        for part in range(2):
+            x_of = [top_along_x(member, x, part, 1) for member in range(3)]
+            z_of = [top_along_z(member, x, part, 1) for member in range(3)]
+            shear = top_at(11, x, part)
+            volume = top_at(10, x, part) * (x_of[0] + y_of[1][part] + z_of[2])
+            twice = shear + shear
+            change = (
+                volume + twice * x_of[0],
+                volume + twice * y_of[1][part],
+                volume + twice * z_of[2],
+                shear * (y_of[0][part] + x_of[1]),
+                shear * (z_of[0] + x_of[2]),
+                shear * (z_of[1] + y_of[2][part]),
+            )
+            for k in range(6):
+                top[SXX + k, x, part, pl.ds(8, 8), :] = top_at(SXX + k, x, part) + change[k]
+
+    def top_layers(update, begin, end, *more):
+        def layer(x, carry):
+            update(x, *more)
+            return carry
+
+        lax.fori_loop(begin, end, layer, 0)
+
     load_stress.wait()
 
     edges[...] = jnp.zeros(edges.shape, F32)
@@ -419,6 +620,21 @@
         return carry
 
     lax.fori_loop(0, cells_x, pack_first, 0)
+
+    load_material.wait()
+
+    def widen(cell, carry):
+        for k in range(3):
+            coef[k, cell] = TIME_SOIL * raw[k, cell].astype(F32)
+        return carry
+
+    lax.fori_loop(0, cells_x, widen, 0)
+    load_velocity.wait()
+    rims[...] = jnp.zeros(rims.shape, F32)
+    lax.fori_loop(0, cells_x, pack_rims, 0)
+    pl.semaphore_wait(barrier, n_gx + n_gy + 2)
+    sent_top = send_top()
+    sent = send_x(0, soil, 0, first, stress_groups, 2, 1)
     sent += send_y(0)
 
     source = iota((256, 256), 0) & 127
@@ -430,24 +646,6 @@
         minus = source == wanted + forward - 1 - reach
         band[forward] = jnp.where(plus, 1.0, jnp.where(minus, -1.0, 0.0)).astype(BF16)
 
-    load_material.wait()
-
-    def widen(cell, carry):
-        for k in range(3):
-            coef[k, cell] = TIME_SOIL * raw[k, cell].astype(F32)
-        return carry
-
-    lax.fori_loop(0, cells_x, widen, 0)
-    load_velocity.wait()
-
-    finish(sent)
-    outside_zero_x(first, (SXX, SXY, SXZ), 2, 1)
-    prepare(0, False)
-
-    velocity_layers(0, first, SXX, first, vel_a, 0, 3)
-    sent = send_x(1, vel_a, COL, vel_a, move_groups, 1, 2)
-    velocity_layers(0, first, SXX, first, vel_a, 3, cells_x)
-    sent += send_y(1)
 
     for copy in load_small:
         copy.wait()
@@ -533,24 +731,13 @@
     for b in range(buildings):
         internal_forces(b)
 
-    finish(sent)
-    outside_zero_x(vel_a, (0, 1, 2), 1, 2)
-    prepare(1, True)
-
-    stress_layers(1, vel_a, first, SXX, str_a, COL, ROW, 0, 3, True)
-    sent = send_x(2, str_a, COL, str_a, inner_groups, 2, 1)
-    stress_layers(1, vel_a, first, SXX, str_a, COL, ROW, 3, cells_x, True)
-    sent += send_y(2)
-    finish(sent)
-    outside_zero_x(str_a, (0, 3, 4), 2, 1)
-    prepare(2, False)
-
-    velocity_layers(2, str_a, 0, vel_a, vel_b, 0, 3, moved_out)
-    sent_x = send_x(3, vel_b, COL, vel_b, move_groups, 1, 2)
-    velocity_layers(2, str_a, 0, vel_a, vel_b, 3, cells_x, moved_out)
-    sent_y = send_y(3)
-
-    surface = [vel_b[k, inner, ROW, :] for k in range(3)]
+    finish(sent_top)
+    unpack_rims()
+    top_layers(top_velocity, LOW - 3, LOW + cells_x + 3, 2)
+    top_layers(top_stress, LOW - 2, LOW + cells_x + 1)
+    top_layers(top_velocity, LOW, LOW + cells_x, 1)
+
+    surface = [top[k, pl.ds(LOW, cells_x), 0, 8, :] for k in range(3)]
     dash = dashpot[...]
     terms = [dash * surface[0], dash * surface[1], dash * surface[2], dash]
     bid = bids[...]
@@ -590,14 +777,26 @@
 
     gathering = gather_along_gy(0, mine)
 
-    finish(sent_y)
-    prepare(3, True)
-    stress_layers(3, vel_b, str_a, 0, str_b, 0, 0, 3, cells_x, False)
+    finish(sent)
+    outside_zero_x(first, (SXX, SXY, SXZ), 2, 1)
+    prepare(0, False)
+
+    velocity_layers(0, first, SXX, first, vel_a, 0, 3)
+    sent = send_x(1, vel_a, COL, vel_a, move_groups, 1, 2)
+    velocity_layers(0, first, SXX, first, vel_a, 3, cells_x)
+    sent += send_y(1)
+
     finish(gathering)
     gathering = gather_along_gx(0)
-    finish(sent_x)
-    outside_zero_x(vel_b, (0, 1, 2), 1, 2)
-    stress_layers(3, vel_b, str_a, 0, str_b, 0, 0, 0, 3, False)
+
+    finish(sent)
+    outside_zero_x(vel_a, (0, 1, 2), 1, 2)
+    prepare(1, True)
+
+    stress_layers(1, vel_a, first, SXX, str_a, COL, ROW, 0, 3, True)
+    sent = send_x(2, str_a, COL, str_a, inner_groups, 2, 1)
+    stress_layers(1, vel_a, first, SXX, str_a, COL, ROW, 3, cells_x, True)
+    sent += send_y(2)
     finish(gathering)
     arrived = rows_all[0].reshape(n_dev, 128)
     owned = jnp.sum(jnp.where(owners[...] == me, arrived, 0.0), axis=0, keepdims=True)
@@ -630,13 +829,31 @@
         back = jnp.where(small_lane == small_row * buildings + b, whole, back)
     back = jnp.where(small_row < 3, back, 0.0)
     gathering = gather_along_gy(1, jnp.sum(back, axis=0, keepdims=True))
+
+    finish(sent)
+    outside_zero_x(str_a, (0, 3, 4), 2, 1)
+    prepare(2, False)
+
+    velocity_layers(2, str_a, 0, vel_a, vel_b, 0, 3, moved_out)
+    sent_x = send_x(3, vel_b, COL, vel_b, move_groups, 1, 2)
+    velocity_layers(2, str_a, 0, vel_a, vel_b, 3, cells_x, moved_out)
+    sent_y = send_y(3)
+
     for b in range(buildings):
         piece = pl.ds(b * 128, 128)
         disp_out[:, piece] = disp[b][0:6]
         vel_out[:, piece] = vel[b][0:6]
-    wanted = owners[pl.ds(me, 1), :]
     finish(gathering)
     gathering = gather_along_gx(1)
+
+    finish(sent_y)
+    prepare(3, True)
+    stress_layers(3, vel_b, str_a, 0, str_b, 0, 0, 3, cells_x, False)
+    finish(sent_x)
+    outside_zero_x(vel_b, (0, 1, 2), 1, 2)
+    stress_layers(3, vel_b, str_a, 0, str_b, 0, 0, 0, 3, False)
+
+    wanted = owners[pl.ds(me, 1), :]
     finish(gathering)
     arrived = rows_all[1].reshape(n_dev, 128)
     held = jnp.where(iota((n_dev, 128), 0) == wanted, arrived, 0.0)
@@ -712,6 +929,9 @@
             pltpu.VMEM((4, 3, cells_x // 4, 8, 128), F32),
             pltpu.VMEM((4, 3, cells_x // 4, 8, 128), F32),
             pltpu.VMEM((4, 3, cells_x // 4, 8, 128), F32),
+            pltpu.VMEM((12, cells_x + LOW + HIGH, 2, 24, 128), F32),
+            pltpu.VMEM((12, 8, 128), F32),
+            pltpu.VMEM((3, 2, 12, 8, 128), F32),
             pltpu.VMEM((n_dev, 128), jnp.int32),
             pltpu.VMEM((8, 128), jnp.int32),
             pltpu.VMEM((2, buildings, 8, 128), F32),
@@ -732,6 +952,8 @@
             dma((2, n_gy - 1)),
             dma((2, n_gx - 1)),
             dma((2, n_gx - 1)),
+            dma((12,)),
+            dma((12,)),
         ],
         compiler_params=pltpu.CompilerParams(
             collective_id=0, has_side_effects=True, vmem_limit_bytes=limit

time: 51.5 us -> 45 us (0.87)
  the two profiles are of different devices: /device:TPU:1 before, /device:TPU:0 now
where the time goes in v2:
time: 45 us; the launch traced here: 44.8 us
  Pallas kernels  44.2 us (98%)
  between operations  0.64 us (1%)
    pallas_call x1, Pallas kernels, shards(): pl.pallas_call(functools.partial(kernel, n_gx, n_gy), out_shape=kept, in_...  42.7 us
    pallas_call x1, Pallas kernels, shards(): pl.pallas_call(write_out, out_shape=(jax.ShapeDtypeStruct(soil.shape, F32...  1.45 us

profile of v2, /device:TPU:0, one launch (start us, length us, event | category | flops | bytes accessed | tf_op | source)
XLA Modules:
  0.0 44.8 jit_solution(16444555656038190458)
XLA Ops:
  0.6 42.7 %shard_map.138 = (f32[3,8,64,128]{3,2,1,0:T(8,128)S(1)}, f32[6,8,64,128]{3,2,1,0:T(8,128)S(1)}, f32[3,8,128]{2,1,0:T(8,128)S(1)}, f32[6,1024]{1,0:T(8,128)S(1)}, f32[6,1024]{1,0:T(8,128)S(1)}) custom-call(f32[9,8,64,128]{3,2,1,0:T(8,128)} %soil.1, bf16[3,8,64,128]{3,2,1,0:T(8,128)(2,1)} %material.1, f32[8,128]{1,0:T(8,128)} %hbm_dashpot.1, ...), custom_call_target="tpu_custom_call" | custom-call | tf_op jit(solution)/shard_map/pallas_call | solution.py:905
  43.4 1.5 %shard_map.139 = (f32[9,8,64,128]{3,2,1,0:T(8,128)}, f32[3,8,128]{2,1,0:T(8,128)}, f32[6,1024]{1,0:T(8,128)}, f32[6,1024]{1,0:T(8,128)}) custom-call(f32[3,8,64,128]{3,2,1,0:T(8,128)S(1)} %get-tuple-element.9.moved, f32[6,8,64,128]{3,2,1,0:T(8,128)S(1)} %get-tuple-element.10.stress, f32[3,8,128]{2,1,0:T(8,128)S(1)} %get-tuple-element.11.force, ...), custom_call_target="tpu_custom_call" | custom-call | tf_op jit(solution)/shard_map/pallas_call | solution.py:962

commit v3 on v2

--- a/solution.py
+++ b/solution.py
@@ -17,6 +17,8 @@
 ROW = 8
 COL = 2
 LOW, HIGH = 5, 4
+RIM = LOW + HIGH
+SLOTS = 128 // RIM
 F32 = jnp.float32
 BF16 = jnp.bfloat16
 
@@ -424,20 +426,29 @@
     inner_groups = ((0, 0, 1), (3, 3, 2))
     move_groups = ((0, 0, 3),)
 
-    fields = rims.shape[0]
-    wide_lane = lane
-
-    def pack_rims(cell, carry):
+    fields = top.shape[0]
+
+    def top_own(cell, carry):
         for member in range(fields):
             if member < 9:
                 value = at(first, member, cell + COL, ROW)
             else:
                 value = coef[member - 9, cell, pl.ds(0, 8), :]
             top[member, cell + LOW, 0, pl.ds(8, 8), :] = value
-            rims[member] = jnp.where(
-                wide_lane >> 4 == cell, rolled(value, (16 * cell + LOW) & 127), rims[member]
-            )
         return carry
+
+    def pack_rims():
+        packed = None
+        for slot_id in range(fields * cells_x):
+            member, cell = divmod(slot_id, cells_x)
+            begin = RIM * (slot_id % SLOTS)
+            value = rolled(top[member, cell + LOW, 0, pl.ds(8, 8), :], (begin + LOW) % 128)
+            packed = value if begin == 0 else jnp.where(lane < begin, packed, value)
+            if slot_id % SLOTS == SLOTS - 1 or slot_id == fields * cells_x - 1:
+                rims[slot_id // SLOTS] = packed
+
+    rim_tiles = -(-fields * cells_x // SLOTS)
+    corner_tiles = -(-(fields - 2) * cells_x // SLOTS)
 
     def send_top():
         copies = []
@@ -468,12 +479,12 @@
             )
         for k, (device, row, column, size) in enumerate(
             (
-                ({"gx": gx_up, "gy": gy_up}, 0, 0, fields - 2),
-                ({"gx": gx_up, "gy": gy_down}, 0, 1, fields - 2),
-                ({"gx": gx_down, "gy": gy_up}, 2, 0, fields - 2),
-                ({"gx": gx_down, "gy": gy_down}, 2, 1, fields - 2),
-                ({"gy": gy_up}, 1, 0, fields),
-                ({"gy": gy_down}, 1, 1, fields),
+                ({"gx": gx_up, "gy": gy_up}, 0, 0, corner_tiles),
+                ({"gx": gx_up, "gy": gy_down}, 0, 1, corner_tiles),
+                ({"gx": gx_down, "gy": gy_up}, 2, 0, corner_tiles),
+                ({"gx": gx_down, "gy": gy_down}, 2, 1, corner_tiles),
+                ({"gy": gy_up}, 1, 0, rim_tiles),
+                ({"gy": gy_down}, 1, 1, rim_tiles),
             )
         ):
             copies.append(
@@ -488,40 +499,30 @@
         return copies
 
     def unpack_rims():
-        spot = wide_lane & 15
-
-        def fill(row, member, shown, x, cell):
-            low = jnp.where(shown & (gy > 0), rims_in[row, 0, member], 0.0)
-            high = jnp.where(shown & (gy < n_gy - 1), rims_in[row, 1, member], 0.0)
-            both = jnp.where(spot < LOW, low, high)
-            both = rolled(both, (256 - LOW - 16 * cell) & 127)
-            near = (wide_lane < HIGH) | (wide_lane >= 128 - LOW)
-            top[member, x, 1, pl.ds(8, 8), :] = jnp.where(near, both, 0.0)
-
-        def layer_inside(cell, carry):
-            for member in range(fields):
-                fill(1, member, True, cell + LOW, cell)
-            return carry
-
-        lax.fori_loop(0, cells_x, layer_inside, 0)
-
-        def layer_low(x, carry):
-            for member in range(fields - 2):
-                fill(0, member, gx > 0, x, x + cells_x - LOW)
-            for member in range(fields - 2, fields):
-                top[member, x, 1, pl.ds(8, 8), :] = zero_tile
-            return carry
-
-        lax.fori_loop(0, LOW, layer_low, 0)
-
-        def layer_high(cell, carry):
-            for member in range(fields - 2):
-                fill(2, member, gx < n_gx - 1, cell + LOW + cells_x, cell)
-            for member in range(fields - 2, fields):
-                top[member, cell + LOW + cells_x, 1, pl.ds(8, 8), :] = zero_tile
-            return carry
-
-        lax.fori_loop(0, HIGH, layer_high, 0)
+        spot = lane - RIM * ((lane * 57) >> 9)
+        near = (lane < HIGH) | (lane >= 128 - LOW)
+
+        for row, tiles, members, cells, shown in (
+            (1, rim_tiles, fields, range(cells_x), True),
+            (0, corner_tiles, fields - 2, range(cells_x - LOW, cells_x), gx > 0),
+            (2, corner_tiles, fields - 2, range(HIGH), gx < n_gx - 1),
+        ):
+            both = []
+            for tile in range(tiles):
+                low = jnp.where(shown & (gy > 0), rims_in[row, 0, tile], 0.0)
+                high = jnp.where(shown & (gy < n_gy - 1), rims_in[row, 1, tile], 0.0)
+                both.append(jnp.where(spot < LOW, low, high))
+            for cell in cells:
+                x = cell + LOW + (row - 1) * cells_x
+                for member in range(fields):
+                    if member < members:
+                        slot_id = member * cells_x + cell
+                        begin = RIM * (slot_id % SLOTS)
+                        value = rolled(both[slot_id // SLOTS], (256 - LOW - begin) % 128)
+                        value = jnp.where(near, value, 0.0)
+                    else:
+                        value = zero_tile
+                    top[member, x, 1, pl.ds(8, 8), :] = value
 
         def outside(x, carry):
             for member in range(fields):
@@ -544,7 +545,7 @@
 
         def moved(shift):
             mine, other = [rolled(part, shift & 127) for part in parts]
-            across = wide_lane < shift if shift > 0 else wide_lane >= 128 + shift
+            across = lane < shift if shift > 0 else lane >= 128 + shift
             return jnp.where(across, other, mine), jnp.where(across, mine, other)
 
         if forward:
@@ -601,12 +602,13 @@
             for k in range(6):
                 top[SXX + k, x, part, pl.ds(8, 8), :] = top_at(SXX + k, x, part) + change[k]
 
-    def top_layers(update, begin, end, *more):
-        def layer(x, carry):
-            update(x, *more)
+    def top_layers(update, begin, size, groups, *more):
+        def layers(i, carry):
+            for k in range(size):
+                update(begin + i * size + k, *more)
             return carry
 
-        lax.fori_loop(begin, end, layer, 0)
+        lax.fori_loop(0, groups, layers, 0)
 
     load_stress.wait()
 
@@ -630,13 +632,6 @@
 
     lax.fori_loop(0, cells_x, widen, 0)
     load_velocity.wait()
-    rims[...] = jnp.zeros(rims.shape, F32)
-    lax.fori_loop(0, cells_x, pack_rims, 0)
-    pl.semaphore_wait(barrier, n_gx + n_gy + 2)
-    sent_top = send_top()
-    sent = send_x(0, soil, 0, first, stress_groups, 2, 1)
-    sent += send_y(0)
-
     source = iota((256, 256), 0) & 127
     column = iota((256, 256), 1)
     wanted = column & 127
@@ -731,11 +726,22 @@
     for b in range(buildings):
         internal_forces(b)
 
+    lax.fori_loop(0, cells_x, top_own, 0)
+    pack_rims()
+    pl.semaphore_wait(barrier, n_gx + n_gy + 2)
+    sent_y = send_y(0)
+    sent_top = send_top()
+    sent_x = send_x(0, soil, 0, first, stress_groups, 2, 1)
+
+    finish(sent_y)
+    prepare(0, False)
+    velocity_layers(0, first, SXX, first, vel_a, 3, cells_x)
+
     finish(sent_top)
     unpack_rims()
-    top_layers(top_velocity, LOW - 3, LOW + cells_x + 3, 2)
-    top_layers(top_stress, LOW - 2, LOW + cells_x + 1)
-    top_layers(top_velocity, LOW, LOW + cells_x, 1)
+    top_layers(top_velocity, LOW - 3, 7, (cells_x + 6) // 7, 2)
+    top_layers(top_stress, LOW - 2, 4, (cells_x + 4) // 4)
+    top_layers(top_velocity, LOW, 4, cells_x // 4, 1)
 
     surface = [top[k, pl.ds(LOW, cells_x), 0, 8, :] for k in range(3)]
     dash = dashpot[...]
@@ -749,6 +755,14 @@
     sums = jnp.concatenate(sums + [jnp.zeros((128 - len(sums), 128), F32)], 0)
     mine = jnp.sum(sums.T, axis=0, keepdims=True)
 
+    def far_first(count, ring):
+        outer = count // ring
+
+        def hops(k):
+            return min(k // ring, outer - k // ring) + (min(k % ring, ring - k % ring) if ring > 2 else 0)
+
+        return sorted(range(1, count), key=lambda k: -hops(k))
+
     def gather_along_gy(turn, value):
         row_buf[turn, gy] = value
         return [
@@ -759,7 +773,7 @@
                 a_recv.at[turn, k - 1],
                 {"gy": lax.rem(gy + k, n_gy)},
             )
-            for k in range(1, n_gy)
+            for k in far_first(n_gy, 4)
         ]
 
     def gather_along_gx(turn):
@@ -772,18 +786,15 @@
                 b_recv.at[turn, k - 1],
                 {"gx": lax.rem(gx + k, n_gx)},
             )
-            for k in range(1, n_gx)
+            for k in far_first(n_gx, 2)
         ]
 
     gathering = gather_along_gy(0, mine)
 
-    finish(sent)
+    finish(sent_x)
     outside_zero_x(first, (SXX, SXY, SXZ), 2, 1)
-    prepare(0, False)
-
     velocity_layers(0, first, SXX, first, vel_a, 0, 3)
     sent = send_x(1, vel_a, COL, vel_a, move_groups, 1, 2)
-    velocity_layers(0, first, SXX, first, vel_a, 3, cells_x)
     sent += send_y(1)
 
     finish(gathering)
@@ -930,8 +941,8 @@
             pltpu.VMEM((4, 3, cells_x // 4, 8, 128), F32),
             pltpu.VMEM((4, 3, cells_x // 4, 8, 128), F32),
             pltpu.VMEM((12, cells_x + LOW + HIGH, 2, 24, 128), F32),
-            pltpu.VMEM((12, 8, 128), F32),
-            pltpu.VMEM((3, 2, 12, 8, 128), F32),
+            pltpu.VMEM((-(-12 * cells_x // SLOTS), 8, 128), F32),
+            pltpu.VMEM((3, 2, -(-12 * cells_x // SLOTS), 8, 128), F32),
             pltpu.VMEM((n_dev, 128), jnp.int32),
             pltpu.VMEM((8, 128), jnp.int32),
             pltpu.VMEM((2, buildings, 8, 128), F32),

time: 45 us -> 40.7 us (0.904)
  Pallas kernels: 44.2 us -> 40 us
    pallas_call x1, Pallas kernels: 42.7 us -> 38.5 us  [shards(): pl.pallas_call(functools.partial(kernel, n_gx, n_gy), out_shape=kept, in_...]
where the time goes in v3:
time: 40.7 us; the launch traced here: 40.6 us
  Pallas kernels  40 us (98%)
  between operations  0.64 us (2%)
    pallas_call x1, Pallas kernels, shards(): pl.pallas_call(functools.partial(kernel, n_gx, n_gy), out_shape=kept, in_...  38.5 us
    pallas_call x1, Pallas kernels, shards(): pl.pallas_call(write_out, out_shape=(jax.ShapeDtypeStruct(soil.shape, F32...  1.45 us

profile of v3, /device:TPU:0, one launch (start us, length us, event | category | flops | bytes accessed | tf_op | source)
XLA Modules:
  0.0 40.6 jit_solution(17858399409729697690)
XLA Ops:
  0.6 38.5 %shard_map.138 = (f32[3,8,64,128]{3,2,1,0:T(8,128)S(1)}, f32[6,8,64,128]{3,2,1,0:T(8,128)S(1)}, f32[3,8,128]{2,1,0:T(8,128)S(1)}, f32[6,1024]{1,0:T(8,128)S(1)}, f32[6,1024]{1,0:T(8,128)S(1)}) custom-call(f32[9,8,64,128]{3,2,1,0:T(8,128)} %soil.1, bf16[3,8,64,128]{3,2,1,0:T(8,128)(2,1)} %material.1, f32[8,128]{1,0:T(8,128)} %hbm_dashpot.1, ...), custom_call_target="tpu_custom_call" | custom-call | tf_op jit(solution)/shard_map/pallas_call | solution.py:916
  39.1 1.5 %shard_map.139 = (f32[9,8,64,128]{3,2,1,0:T(8,128)}, f32[3,8,128]{2,1,0:T(8,128)}, f32[6,1024]{1,0:T(8,128)}, f32[6,1024]{1,0:T(8,128)}) custom-call(f32[3,8,64,128]{3,2,1,0:T(8,128)S(1)} %get-tuple-element.9.moved, f32[6,8,64,128]{3,2,1,0:T(8,128)S(1)} %get-tuple-element.10.stress, f32[3,8,128]{2,1,0:T(8,128)S(1)} %get-tuple-element.11.force, ...), custom_call_target="tpu_custom_call" | custom-call | tf_op jit(solution)/shard_map/pallas_call | solution.py:973

commit v4 on v3

--- a/solution.py
+++ b/solution.py
@@ -361,6 +361,18 @@
             at(ref, member, x, row + shift - 2),
         )
 
+    def grouped(layer, begin, end):
+        odd = (end - begin) % 2
+        if odd:
+            layer(jnp.int32(begin), 0)
+
+        def pair(i, carry):
+            layer(begin + odd + 2 * i, carry)
+            layer(begin + odd + 2 * i + 1, carry)
+            return carry
+
+        lax.fori_loop(0, (end - begin) // 2, pair, 0)
+
     def velocity_layers(stage, stress, base, old, new, begin, end, out=None):
         sxx, syy, szz, sxy, sxz, syz = range(base, base + 6)
 
@@ -387,7 +399,7 @@
             pack(stage + 1, results, cell)
             return carry
 
-        lax.fori_loop(begin, end, layer, 0)
+        grouped(layer, begin, end)
 
     def stress_layers(stage, moving, stress, base, new, new_x, new_row, begin, end, packing):
         def layer(i, carry):
@@ -420,7 +432,7 @@
                 pack(stage + 1, results, cell)
             return carry
 
-        lax.fori_loop(begin, end, layer, 0)
+        grouped(layer, begin, end)
 
     stress_groups = ((SXX, SXX, 1), (SXY, SXY, 2))
     inner_groups = ((0, 0, 1), (3, 3, 2))

time: 40.7 us -> 37.9 us (0.931)
  the two profiles are of different devices: /device:TPU:0 before, /device:TPU:1 now
where the time goes in v4:
time: 37.9 us; the launch traced here: 37.8 us
  Pallas kernels  37.2 us (98%)
  between operations  0.64 us (2%)
    pallas_call x1, Pallas kernels, shards(): pl.pallas_call(functools.partial(kernel, n_gx, n_gy), out_shape=kept, in_...  35.7 us
    pallas_call x1, Pallas kernels, shards(): pl.pallas_call(write_out, out_shape=(jax.ShapeDtypeStruct(soil.shape, F32...  1.45 us

profile of v4, /device:TPU:1, one launch (start us, length us, event | category | flops | bytes accessed | tf_op | source)
XLA Modules:
  0.0 37.8 jit_solution(6428048408593921622)
XLA Ops:
  0.6 35.7 %shard_map.138 = (f32[3,8,64,128]{3,2,1,0:T(8,128)S(1)}, f32[6,8,64,128]{3,2,1,0:T(8,128)S(1)}, f32[3,8,128]{2,1,0:T(8,128)S(1)}, f32[6,1024]{1,0:T(8,128)S(1)}, f32[6,1024]{1,0:T(8,128)S(1)}) custom-call(f32[9,8,64,128]{3,2,1,0:T(8,128)} %soil.1, bf16[3,8,64,128]{3,2,1,0:T(8,128)(2,1)} %material.1, f32[8,128]{1,0:T(8,128)} %hbm_dashpot.1, ...), custom_call_target="tpu_custom_call" | custom-call | tf_op jit(solution)/shard_map/pallas_call | solution.py:928
  36.4 1.5 %shard_map.139 = (f32[9,8,64,128]{3,2,1,0:T(8,128)}, f32[3,8,128]{2,1,0:T(8,128)}, f32[6,1024]{1,0:T(8,128)}, f32[6,1024]{1,0:T(8,128)}) custom-call(f32[3,8,64,128]{3,2,1,0:T(8,128)S(1)} %get-tuple-element.9.moved, f32[6,8,64,128]{3,2,1,0:T(8,128)S(1)} %get-tuple-element.10.stress, f32[3,8,128]{2,1,0:T(8,128)S(1)} %get-tuple-element.11.force, ...), custom_call_target="tpu_custom_call" | custom-call | tf_op jit(solution)/shard_map/pallas_call | solution.py:985

commit v5 on v4

--- a/solution.py
+++ b/solution.py
@@ -738,6 +738,10 @@
     for b in range(buildings):
         internal_forces(b)
 
+    dash = dashpot[...]
+    bid = bids[...]
+    stands = [jnp.where(bid == b, dash, 0.0) for b in range(buildings)]
+    damping = [jnp.sum(value, axis=0, keepdims=True) for value in stands]
     lax.fori_loop(0, cells_x, top_own, 0)
     pack_rims()
     pl.semaphore_wait(barrier, n_gx + n_gy + 2)
@@ -756,14 +760,12 @@
     top_layers(top_velocity, LOW, 4, cells_x // 4, 1)
 
     surface = [top[k, pl.ds(LOW, cells_x), 0, 8, :] for k in range(3)]
-    dash = dashpot[...]
-    terms = [dash * surface[0], dash * surface[1], dash * surface[2], dash]
-    bid = bids[...]
     sums = [
-        jnp.sum(jnp.where(bid == b, term, 0.0), axis=0, keepdims=True)
-        for term in terms
+        jnp.sum(stands[b] * surface[k], axis=0, keepdims=True)
+        for k in range(3)
         for b in range(buildings)
     ]
+    sums += damping
     sums = jnp.concatenate(sums + [jnp.zeros((128 - len(sums), 128), F32)], 0)
     mine = jnp.sum(sums.T, axis=0, keepdims=True)
 

time: 37.9 us -> 37.9 us (level)
  no operation moved by 1% of the time
where the time goes in v5:
time: 37.9 us; the launch traced here: 37.8 us
  Pallas kernels  37.2 us (98%)
  between operations  0.64 us (2%)
    pallas_call x1, Pallas kernels, shards(): pl.pallas_call(functools.partial(kernel, n_gx, n_gy), out_shape=kept, in_...  35.7 us
    pallas_call x1, Pallas kernels, shards(): pl.pallas_call(write_out, out_shape=(jax.ShapeDtypeStruct(soil.shape, F32...  1.45 us

profile of v5, /device:TPU:1, one launch (start us, length us, event | category | flops | bytes accessed | tf_op | source)
XLA Modules:
  0.0 37.8 jit_solution(8982643455646158386)
XLA Ops:
  0.6 35.7 %shard_map.138 = (f32[3,8,64,128]{3,2,1,0:T(8,128)S(1)}, f32[6,8,64,128]{3,2,1,0:T(8,128)S(1)}, f32[3,8,128]{2,1,0:T(8,128)S(1)}, f32[6,1024]{1,0:T(8,128)S(1)}, f32[6,1024]{1,0:T(8,128)S(1)}) custom-call(f32[9,8,64,128]{3,2,1,0:T(8,128)} %soil.1, bf16[3,8,64,128]{3,2,1,0:T(8,128)(2,1)} %material.1, f32[8,128]{1,0:T(8,128)} %hbm_dashpot.1, ...), custom_call_target="tpu_custom_call" | custom-call | tf_op jit(solution)/shard_map/pallas_call | solution.py:930
  36.4 1.5 %shard_map.139 = (f32[9,8,64,128]{3,2,1,0:T(8,128)}, f32[3,8,128]{2,1,0:T(8,128)}, f32[6,1024]{1,0:T(8,128)}, f32[6,1024]{1,0:T(8,128)}) custom-call(f32[3,8,64,128]{3,2,1,0:T(8,128)S(1)} %get-tuple-element.9.moved, f32[6,8,64,128]{3,2,1,0:T(8,128)S(1)} %get-tuple-element.10.stress, f32[3,8,128]{2,1,0:T(8,128)S(1)} %get-tuple-element.11.force, ...), custom_call_target="tpu_custom_call" | custom-call | tf_op jit(solution)/shard_map/pallas_call | solution.py:987
